TPU v7x, 256 devices: a whole 4x4x8 slice. The times are simulated.
256 devices in a mesh: diag: 32 (over z_lo, x, y), off: 8 (over z_hi, core).
Axes of the slice: x: 4, y: 4, z: 8 (z_hi: 4, z_lo: 2; z = z_hi * 2 + z_lo), core: 2. Of those that a mesh axis runs over, the one named last changes fastest.
Arguments:
- features: bfloat16 [4096, 256], P('diag'), may hold values from -6 to 6
- conv_weight: bfloat16 [2, 3, 256, 128], replicated, may hold values from -0.21875 to 0.21875
- out_weight: bfloat16 [2, 128, 256], replicated, may hold values from -0.5 to 0.5
- proj_weight: bfloat16 [256, 128], replicated, may hold values from -0.375 to 0.375
- offset_embed: bfloat16 [512, 64], P('off'), may hold values from -6 to 6
- pair_filter_weight: bfloat16 [2, 3, 3, 64, 64], replicated, may hold values from -0.25 to 0.25
- head_weight: float32 [64], replicated, may hold values from -0.75 to 0.75
- target: float32 [512, 4096], P('off', 'diag'), may hold values from -6 to 6
- cell_mask: int32 [512, 4096], P('off', 'diag'), may hold values 0 or 1
Outputs:
- prediction: float32 [512, 4096], P('off', 'diag')
- loss: float32 [], replicated
All inputs are finite; a program needn't handle non-finite values. No bound on the sum of `cell_mask` on one device may be relied on, other than what follows from the above.
Results may differ from a plain program's by a relative error of at most 0.008.
Values may be sent and summed in bfloat16 or wider, within the bound.
A program may use at most 128 MiB of HBM per device.

v0:
```python
import jax
import jax.numpy as jnp
from jax import lax
from jax.sharding import PartitionSpec as P

CP = 64
BAND = 512
FIRST_DILATION = 4
SECOND_DILATION = 8
PAIR_DILATION = 4


def with_halo(block, sides, width):
    for axis, dim in sides:
        count = lax.axis_size(axis)
        forward = [(i, i + 1) for i in range(count - 1)]
        backward = [(target, source) for source, target in forward]
        low = lax.ppermute(
            lax.slice_in_dim(block, block.shape[dim] - width, None, axis=dim), axis, forward
        )
        high = lax.ppermute(lax.slice_in_dim(block, 0, width, axis=dim), axis, backward)
        block = jnp.concatenate([low, block, high], axis=dim)
    return block


def passed_along(block, axis, distance):
    devices = range(lax.axis_size(axis))
    route = [(i - distance, i) for i in devices if i - distance in devices]
    return lax.ppermute(block, axis, route)


def filter_taps(field, weight, spread_rows):
    chans, rows_off, rows_bin = field.shape
    out_off = rows_off - 2 * spread_rows
    out_bin = rows_bin - 2 * spread_rows
    accum = jnp.zeros((weight.shape[2], out_off * out_bin), jnp.float32)
    for tap_off in range(3):
        for tap_bin in range(3):
            piece = field[
                :,
                tap_off * spread_rows : tap_off * spread_rows + out_off,
                tap_bin * spread_rows : tap_bin * spread_rows + out_bin,
            ]
            piece = piece.reshape(chans, out_off * out_bin)
            accum = accum + jnp.dot(
                weight[tap_off, tap_bin], piece, preferred_element_type=jnp.float32
            )
    return accum.reshape(weight.shape[2], out_off, out_bin)


def trunk_layer(rows, padded, conv, outw, spread_rows):
    count = rows.shape[0]
    accum = jnp.zeros((count, conv.shape[2]), jnp.float32)
    for tap in range(3):
        accum = accum + jnp.dot(
            padded[tap * spread_rows : tap * spread_rows + count],
            conv[tap],
            preferred_element_type=jnp.float32,
        )
    interior = jax.nn.relu(accum).astype(jnp.bfloat16)
    return (
        rows.astype(jnp.float32) + jnp.dot(interior, outw, preferred_element_type=jnp.float32)
    ).astype(jnp.bfloat16)


def pair_edges(field, spread_rows):
    return with_halo(field, (("diag", 2), ("off", 1)), spread_rows)


def body(
    features,
    conv_weight,
    out_weight,
    proj_weight,
    offset_embed,
    pair_filter_weight,
    head_weight,
    target,
    cell_mask,
):
    local_bins = features.shape[0]
    diag_count = lax.axis_size("diag")
    off_count = lax.axis_size("off")
    diag_index = lax.axis_index("diag")
    off_index = lax.axis_index("off")
    total_bins = local_bins * diag_count
    hidden = features
    for layer_apply, spread_rows in enumerate((FIRST_DILATION, SECOND_DILATION)):
        padded = with_halo(jax.nn.relu(hidden), (("diag", 0),), spread_rows)
        hidden = trunk_layer(
            hidden, padded, conv_weight[layer_apply], out_weight[layer_apply], spread_rows
        )
    projected = jnp.dot(hidden, proj_weight, preferred_element_type=jnp.float32).astype(
        jnp.bfloat16
    )
    left = projected[:, :CP]
    right = projected[:, CP:]
    reach = (local_bins + BAND - 2) // local_bins
    pieces = [right]
    for ahead in range(1, reach + 1):
        pieces.append(passed_along(right, "diag", -ahead))
    window_all = jnp.concatenate(pieces, 0)
    width = BAND // off_count
    window = lax.dynamic_slice_in_dim(window_all, off_index * width, local_bins + width - 1, 0)
    window_t = window.T
    skewed = jnp.stack([window_t[:, offset : offset + local_bins] for offset in range(width)], 1)
    total = (
        skewed.astype(jnp.float32)
        + left.T.astype(jnp.float32)[:, None, :]
        + offset_embed.T.astype(jnp.float32)[:, :, None]
    )
    pair_block = jax.nn.relu(total).astype(jnp.bfloat16)
    spread_rows = PAIR_DILATION
    first_layer = filter_taps(
        pair_edges(pair_block, spread_rows), pair_filter_weight[0], spread_rows
    )
    interior = jax.nn.relu(first_layer).astype(jnp.bfloat16)
    second_layer = filter_taps(
        pair_edges(interior, spread_rows), pair_filter_weight[1], spread_rows
    )
    result = pair_block.astype(jnp.float32) + second_layer
    prediction = jnp.sum(result * head_weight[:, None, None], 0)
    global_bins = diag_index * local_bins + jnp.arange(local_bins, dtype=jnp.int32)
    global_offs = off_index * width + jnp.arange(width, dtype=jnp.int32)
    within = global_offs[:, None] + global_bins[None, :] < total_bins
    valid = cell_mask.astype(jnp.float32) * within.astype(jnp.float32)
    partial_err = jnp.sum(valid * (prediction - target) ** 2)
    summed = lax.psum(partial_err, ("diag", "off"))
    loss = summed / (BAND * total_bins)
    return (prediction, loss)


def solution(mesh):
    in_specs = (
        P("diag", None),
        P(),
        P(),
        P(),
        P("off", None),
        P(),
        P(),
        P("off", "diag"),
        P("off", "diag"),
    )
    out_specs = (P("off", "diag"), P())
    return jax.shard_map(body, mesh=mesh, in_specs=in_specs, out_specs=out_specs, check_vma=False)
```

profile of v0, /device:TPU:1, one launch (start us, length us, event | category | flops | bytes accessed | tf_op | source)
XLA Modules:
  0.0 222.5 jit_solution(14228484610260879465)
XLA Ops:
  1.6 1.3 collective-permute-start.1
  2.9 4.7 %collective-permute-start = (bf16[4,256]{1,0:T(4,128)(2,1)S(1)}, bf16[4,256]{1,0:T(4,128)(2,1)S(1)}, u32[]{:S(2)}, u32[]{:S(2)}) collective-permute-start(bf16[4,256]{1,0:T(4,128)(2,1)S(1)} %get-tuple-element.34), channel_id=1, source_target_pairs={{0,8},{8,16},{16,24},{24,32},{32,40},{40,48},{48,56},{56,64},{64,7... | collective-permute-start | bytes 6152 | tf_op jit(solution)/shard_map/ppermute | solution.py:18
  11.8 1.3 collective-permute-start.3
  13.1 4.0 %collective-permute-start.2 = (bf16[8,256]{1,0:T(8,128)(2,1)S(1)}, bf16[8,256]{1,0:T(8,128)(2,1)S(1)}, u32[]{:S(2)}, u32[]{:S(2)}) collective-permute-start(bf16[8,256]{1,0:T(8,128)(2,1)S(1)} %get-tuple-element.32), channel_id=1, source_target_pairs={{0,8},{8,16},{16,24},{24,32},{32,40},{40,48},{48,56},{56,64},{64,7... | collective-permute-start | bytes 12296 | tf_op jit(solution)/shard_map/ppermute | solution.py:18
  20.4 1.3 collective-permute-start.4
  21.8 1.3 collective-permute-start.5
  23.1 1.3 collective-permute-start.6
  24.4 1.3 collective-permute-start.7
  25.7 4.5 %collective-permute-done.5 = bf16[128,64]{0,1:T(8,128)(2,1)S(1)} collective-permute-done((bf16[128,64]{0,1:T(8,128)(2,1)S(1)}, bf16[128,64]{0,1:T(8,128)(2,1)S(1)}, u32[]{:S(2)}, u32[]{:S(2)}) %collective-permute-start.5) | collective-permute-done | bytes 16416 | tf_op jit(solution)/shard_map/ppermute | solution.py:29
  30.2 4.3 %collective-permute-done.6 = bf16[128,64]{0,1:T(8,128)(2,1)S(1)} collective-permute-done((bf16[128,64]{0,1:T(8,128)(2,1)S(1)}, bf16[128,64]{0,1:T(8,128)(2,1)S(1)}, u32[]{:S(2)}, u32[]{:S(2)}) %collective-permute-start.6) | collective-permute-done | bytes 16416 | tf_op jit(solution)/shard_map/ppermute | solution.py:29
  34.5 3.1 %collective-permute-done.7 = bf16[128,64]{0,1:T(8,128)(2,1)S(1)} collective-permute-done((bf16[128,64]{0,1:T(8,128)(2,1)S(1)}, bf16[128,64]{0,1:T(8,128)(2,1)S(1)}, u32[]{:S(2)}, u32[]{:S(2)}) %collective-permute-start.7) | collective-permute-done | bytes 16416 | tf_op jit(solution)/shard_map/ppermute | solution.py:29
  45.1 1.9 copy.21
  47.0 2.5 %collective-permute-start.8 = (bf16[64,64,4]{1,0,2:T(8,128)(2,1)}, bf16[64,64,4]{1,0,2:T(8,128)(2,1)S(1)}, u32[]{:S(2)}, u32[]{:S(2)}) collective-permute-start(bf16[64,64,4]{1,0,2:T(8,128)(2,1)} %copy.21), channel_id=1, source_target_pairs={{0,8},{8,16},{16,24},{24,32},{32,40},{40,48},{48,56},{56,64},{64,7... | collective-permute-start | bytes 98312 | tf_op jit(solution)/shard_map/ppermute | solution.py:18
  52.1 1.8 copy.23
  53.9 2.9 %collective-permute-done.9 = bf16[64,64,4]{1,0,2:T(8,128)(2,1)} collective-permute-done((bf16[64,64,4]{1,0,2:T(8,128)(2,1)S(1)}, bf16[64,64,4]{1,0,2:T(8,128)(2,1)}, u32[]{:S(2)}, u32[]{:S(2)}) %collective-permute-start.9) | collective-permute-done | bytes 32800 | tf_op jit(solution)/shard_map/ppermute | solution.py:21
  56.8 2.6 %copy.24 = bf16[64,64,4]{2,0,1:T(8,128)(2,1)S(1)} copy(bf16[64,64,4]{1,0,2:T(8,128)(2,1)} %collective-permute-done.9) | data formatting | bytes 65536 | tf_op jit(solution)/shard_map/ppermute | solution.py:21
  59.6 9.0 %collective-permute-start.10 = (bf16[64,4,136]{2,0,1:T(8,128)(2,1)S(1)}, bf16[64,4,136]{2,0,1:T(8,128)(2,1)S(1)}, u32[]{:S(2)}, u32[]{:S(2)}) collective-permute-start(bf16[64,4,136]{2,0,1:T(8,128)(2,1)S(1)} %get-tuple-element.9), channel_id=1, source_target_pairs={{0,1},{1,2},{2,3},{3,4},{4,5},{5,6},{6,7},{8,9},{9,10},{10,11},{11... | collective-permute-start | bytes 208904 | tf_op jit(solution)/shard_map/ppermute | solution.py:18
  68.6 2.1 collective-permute-start.11
  71.9 3.9 %collective-permute-done.11 = bf16[64,4,136]{2,0,1:T(8,128)(2,1)S(1)} collective-permute-done((bf16[64,4,136]{2,0,1:T(8,128)(2,1)S(1)}, bf16[64,4,136]{2,0,1:T(8,128)(2,1)S(1)}, u32[]{:S(2)}, u32[]{:S(2)}) %collective-permute-start.11) | collective-permute-done | bytes 69664 | tf_op jit(solution)/shard_map/ppermute | solution.py:21
  75.8 2.8 %pad_maximum_fusion.1 = (bf16[64,68,136]{2,0,1:T(8,128)(2,1)S(1)}, bf16[64,68,136]{2,0,1:T(8,128)(2,1)S(1)}) fusion(bf16[64,4,136]{2,0,1:T(8,128)(2,1)S(1)} %collective-permute-done.11, bf16[64,64,4]{2,0,1:T(8,128)(2,1)S(1)} %copy.24, bf16[64,64,128]{2,0,1:T(8,128)(2,1)S(1)} %maximum_convert_fusion, bf16[64,64,4]{2,0,1:T(8,128)(2,1)S(1)} %copy.23, ...), kind=kLoop, calls=%fused_computation.24 | loop fusion | flops 9469952 | bytes 3620864 | tf_op jit(solution)/shard_map/concatenate | solution.py:22
  78.6 1.6 slice_bitcast_fusion
  87.6 3.7 %collective-permute-start.12 = (bf16[64,64,4]{1,0,2:T(8,128)(2,1)S(1)}, bf16[64,64,4]{1,0,2:T(8,128)(2,1)S(1)}, u32[]{:S(2)}, u32[]{:S(2)}) collective-permute-start(bf16[64,64,4]{1,0,2:T(8,128)(2,1)S(1)} %copy.41), channel_id=1, source_target_pairs={{0,8},{8,16},{16,24},{24,32},{32,40},{40,48},{48,56},{56,64},{64,7... | collective-permute-start | bytes 98312 | tf_op jit(solution)/shard_map/ppermute | solution.py:18
  91.8 1.3 collective-permute-start.13
  93.7 3.5 %collective-permute-done.13 = bf16[64,64,4]{1,0,2:T(8,128)(2,1)} collective-permute-done((bf16[64,64,4]{1,0,2:T(8,128)(2,1)S(1)}, bf16[64,64,4]{1,0,2:T(8,128)(2,1)}, u32[]{:S(2)}, u32[]{:S(2)}) %collective-permute-start.13) | collective-permute-done | bytes 32800 | tf_op jit(solution)/shard_map/ppermute | solution.py:21
  97.2 1.4 copy.38
  99.0 3.2 %collective-permute-start.14 = (bf16[64,4,136]{2,1,0:T(4,128)(2,1)S(1)}, bf16[64,4,136]{2,1,0:T(4,128)(2,1)S(1)}, u32[]{:S(2)}, u32[]{:S(2)}) collective-permute-start(bf16[64,4,136]{2,1,0:T(4,128)(2,1)S(1)} %get-tuple-element.5), channel_id=1, source_target_pairs={{0,1},{1,2},{2,3},{3,4},{4,5},{5,6},{6,7},{8,9},{9,10},{10,11},{11... | collective-permute-start | bytes 208904 | tf_op jit(solution)/shard_map/ppermute | solution.py:18
  102.2 1.9 collective-permute-start.15
  105.3 6.0 %collective-permute-done.15 = bf16[64,4,136]{2,1,0:T(4,128)(2,1)S(1)} collective-permute-done((bf16[64,4,136]{2,1,0:T(4,128)(2,1)S(1)}, bf16[64,4,136]{2,1,0:T(4,128)(2,1)S(1)}, u32[]{:S(2)}, u32[]{:S(2)}) %collective-permute-start.15) | collective-permute-done | bytes 69664 | tf_op jit(solution)/shard_map/ppermute | solution.py:21
  111.3 3.6 %pad_maximum_fusion = (bf16[64,68,136]{2,1,0:T(8,128)(2,1)S(1)}, bf16[64,68,136]{2,1,0:T(8,128)(2,1)S(1)}) fusion(bf16[64,4,136]{2,1,0:T(4,128)(2,1)S(1)} %collective-permute-done.15, bf16[64,64,4]{2,1,0:T(8,128)(2,1)S(1)} %copy.38, bf16[64,64,128]{2,1,0:T(8,128)(2,1)S(1)} %bitcast.450, bf16[64,64,4]{2,1,0:T(8,128)(2,1)S(1)} %copy.37, ...), kind=kLoop, calls=%fused_computation.22 | loop fusion | flops 9469952 | bytes 3620864 | tf_op jit(solution)/shard_map/concatenate | solution.py:22
  120.4 1.7 fusion.91
  125.2 2.8 %fusion.5 = f32[8192]{0:T(1024)S(1)} fusion(f32[8192,64]{0,1:T(8,128)S(1)} %convolution_add_fusion.1, bf16[8,8,64,128]{3,2,1,0:T(8,128)(2,1)S(1)} %bitcast.454, f32[64]{0:T(128)S(1)} %copy-done.12, bf16[3,3,64,64]{3,2,1,0:T(8,128)(2,1)S(1)} %get-tuple-element.30, f32[64,64]{0,1:T(8,128)S(1)} %convert_bitcast_fusion, f32[64,128]{1,0:T(8,128)S(1)} %get-tuple-element.36, ...), kind=kOutput, calls=%fused_computation.26 | convolution fusion | flops 72343552 | bytes 4309504 | tf_op jit(solution)/shard_map/dot_general | solution.py:45
  128.8 91.9 %psum.7 = f32[]{:T(128)} all-reduce(f32[]{:T(128)} %multiply_reduce_fusion), channel_id=1, replica_groups=mesh['diag'=32,'off'=8] {'diag','off'}, use_global_device_ids=true, to_apply=%region_2.3 | all-reduce | flops 1 | bytes 8 | tf_op jit(solution)/shard_map/psum | solution.py:128
  (151 shorter events, 38.9 us)
Async XLA Ops:
  0.6 19.5 %copy-start = (bf16[256,128]{1,0:T(8,128)(2,1)S(1)}, bf16[256,128]{1,0:T(8,128)(2,1)}, u32[]{:S(2)}) copy-start(bf16[256,128]{1,0:T(8,128)(2,1)} %param.12) | copy-start | bytes 196612
  0.6 19.5 %copy-start.8 = (bf16[2,128,256]{2,1,0:T(8,128)(2,1)S(1)}, bf16[2,128,256]{2,1,0:T(8,128)(2,1)}, u32[]{:S(2)}) copy-start(bf16[2,128,256]{2,1,0:T(8,128)(2,1)} %param.11) | copy-start | bytes 393220
  0.7 21.1 %copy-start.11 = (bf16[64,64]{1,0:T(8,128)(2,1)S(1)}, bf16[64,64]{1,0:T(8,128)(2,1)}, u32[]{:S(2)}) copy-start(bf16[64,64]{1,0:T(8,128)(2,1)} %param.13) | copy-start | bytes 24580
  1.6 8.0 %collective-permute-start.1 = (bf16[4,256]{1,0:T(4,128)(2,1)S(1)}, bf16[4,256]{1,0:T(4,128)(2,1)S(1)}, u32[]{:S(2)}, u32[]{:S(2)}) collective-permute-start(bf16[4,256]{1,0:T(4,128)(2,1)S(1)} %get-tuple-element.35), channel_id=1, source_target_pairs={{8,0},{16,8},{24,16},{32,24},{40,32},{48,40},{56,48},{64,56},{72,6... | collective-permute-start | bytes 6152 | tf_op jit(solution)/shard_map/ppermute | solution.py:21
  2.9 7.7 %collective-permute-start = (bf16[4,256]{1,0:T(4,128)(2,1)S(1)}, bf16[4,256]{1,0:T(4,128)(2,1)S(1)}, u32[]{:S(2)}, u32[]{:S(2)}) collective-permute-start(bf16[4,256]{1,0:T(4,128)(2,1)S(1)} %get-tuple-element.34), channel_id=1, source_target_pairs={{0,8},{8,16},{16,24},{24,32},{32,40},{40,48},{48,56},{56,64},{64,7... | collective-permute-start | bytes 6152 | tf_op jit(solution)/shard_map/ppermute | solution.py:18
  11.8 6.3 %collective-permute-start.3 = (bf16[8,256]{1,0:T(8,128)(2,1)S(1)}, bf16[8,256]{1,0:T(8,128)(2,1)S(1)}, u32[]{:S(2)}, u32[]{:S(2)}) collective-permute-start(bf16[8,256]{1,0:T(8,128)(2,1)S(1)} %get-tuple-element.33), channel_id=1, source_target_pairs={{8,0},{16,8},{24,16},{32,24},{40,32},{48,40},{56,48},{64,56},{72,6... | collective-permute-start | bytes 12296 | tf_op jit(solution)/shard_map/ppermute | solution.py:21
  13.1 6.0 %collective-permute-start.2 = (bf16[8,256]{1,0:T(8,128)(2,1)S(1)}, bf16[8,256]{1,0:T(8,128)(2,1)S(1)}, u32[]{:S(2)}, u32[]{:S(2)}) collective-permute-start(bf16[8,256]{1,0:T(8,128)(2,1)S(1)} %get-tuple-element.32), channel_id=1, source_target_pairs={{0,8},{8,16},{16,24},{24,32},{32,40},{40,48},{48,56},{56,64},{64,7... | collective-permute-start | bytes 12296 | tf_op jit(solution)/shard_map/ppermute | solution.py:18
  20.4 5.2 %collective-permute-start.4 = (bf16[128,64]{0,1:T(8,128)(2,1)S(1)}, bf16[128,64]{0,1:T(8,128)(2,1)S(1)}, u32[]{:S(2)}, u32[]{:S(2)}) collective-permute-start(bf16[128,64]{0,1:T(8,128)(2,1)S(1)} %get-tuple-element.38), channel_id=1, source_target_pairs={{8,0},{16,8},{24,16},{32,24},{40,32},{48,40},{56,48},{64,56},{72,6... | collective-permute-start | bytes 49160 | tf_op jit(solution)/shard_map/ppermute | solution.py:29
  21.8 8.4 %collective-permute-start.5 = (bf16[128,64]{0,1:T(8,128)(2,1)S(1)}, bf16[128,64]{0,1:T(8,128)(2,1)S(1)}, u32[]{:S(2)}, u32[]{:S(2)}) collective-permute-start(bf16[128,64]{0,1:T(8,128)(2,1)S(1)} %get-tuple-element.38), channel_id=1, source_target_pairs={{16,0},{24,8},{32,16},{40,24},{48,32},{56,40},{64,48},{72,56},{80,... | collective-permute-start | bytes 49160 | tf_op jit(solution)/shard_map/ppermute | solution.py:29
  23.1 11.4 %collective-permute-start.6 = (bf16[128,64]{0,1:T(8,128)(2,1)S(1)}, bf16[128,64]{0,1:T(8,128)(2,1)S(1)}, u32[]{:S(2)}, u32[]{:S(2)}) collective-permute-start(bf16[128,64]{0,1:T(8,128)(2,1)S(1)} %get-tuple-element.38), channel_id=1, source_target_pairs={{24,0},{32,8},{40,16},{48,24},{56,32},{64,40},{72,48},{80,56},{88,... | collective-permute-start | bytes 49160 | tf_op jit(solution)/shard_map/ppermute | solution.py:29
  24.4 13.2 %collective-permute-start.7 = (bf16[128,64]{0,1:T(8,128)(2,1)S(1)}, bf16[128,64]{0,1:T(8,128)(2,1)S(1)}, u32[]{:S(2)}, u32[]{:S(2)}) collective-permute-start(bf16[128,64]{0,1:T(8,128)(2,1)S(1)} %get-tuple-element.38), channel_id=1, source_target_pairs={{32,0},{40,8},{48,16},{56,24},{64,32},{72,40},{80,48},{88,56},{96,... | collective-permute-start | bytes 49160 | tf_op jit(solution)/shard_map/ppermute | solution.py:29
  42.9 1.0 copy-start.2
  47.0 5.1 %collective-permute-start.8 = (bf16[64,64,4]{1,0,2:T(8,128)(2,1)}, bf16[64,64,4]{1,0,2:T(8,128)(2,1)S(1)}, u32[]{:S(2)}, u32[]{:S(2)}) collective-permute-start(bf16[64,64,4]{1,0,2:T(8,128)(2,1)} %copy.21), channel_id=1, source_target_pairs={{0,8},{8,16},{16,24},{24,32},{32,40},{40,48},{48,56},{56,64},{64,7... | collective-permute-start | bytes 98312 | tf_op jit(solution)/shard_map/ppermute | solution.py:18
  50.8 6.0 %collective-permute-start.9 = (bf16[64,64,4]{1,0,2:T(8,128)(2,1)S(1)}, bf16[64,64,4]{1,0,2:T(8,128)(2,1)}, u32[]{:S(2)}, u32[]{:S(2)}) collective-permute-start(bf16[64,64,4]{1,0,2:T(8,128)(2,1)S(1)} %copy.22), channel_id=1, source_target_pairs={{8,0},{16,8},{24,16},{32,24},{40,32},{48,40},{56,48},{64,56},{72,6... | collective-permute-start | bytes 98312 | tf_op jit(solution)/shard_map/ppermute | solution.py:21
  59.6 12.3 %collective-permute-start.10 = (bf16[64,4,136]{2,0,1:T(8,128)(2,1)S(1)}, bf16[64,4,136]{2,0,1:T(8,128)(2,1)S(1)}, u32[]{:S(2)}, u32[]{:S(2)}) collective-permute-start(bf16[64,4,136]{2,0,1:T(8,128)(2,1)S(1)} %get-tuple-element.9), channel_id=1, source_target_pairs={{0,1},{1,2},{2,3},{3,4},{4,5},{5,6},{6,7},{8,9},{9,10},{10,11},{11... | collective-permute-start | bytes 208904 | tf_op jit(solution)/shard_map/ppermute | solution.py:18
  68.6 7.2 %collective-permute-start.11 = (bf16[64,4,136]{2,0,1:T(8,128)(2,1)S(1)}, bf16[64,4,136]{2,0,1:T(8,128)(2,1)S(1)}, u32[]{:S(2)}, u32[]{:S(2)}) collective-permute-start(bf16[64,4,136]{2,0,1:T(8,128)(2,1)S(1)} %get-tuple-element.8), channel_id=1, source_target_pairs={{1,0},{2,1},{3,2},{4,3},{5,4},{6,5},{7,6},{9,8},{10,9},{11,10},{12... | collective-permute-start | bytes 208904 | tf_op jit(solution)/shard_map/ppermute | solution.py:21
  81.5 1.2 copy-start.3
  85.4 1.0 copy-start.5
  87.6 5.6 %collective-permute-start.12 = (bf16[64,64,4]{1,0,2:T(8,128)(2,1)S(1)}, bf16[64,64,4]{1,0,2:T(8,128)(2,1)S(1)}, u32[]{:S(2)}, u32[]{:S(2)}) collective-permute-start(bf16[64,64,4]{1,0,2:T(8,128)(2,1)S(1)} %copy.41), channel_id=1, source_target_pairs={{0,8},{8,16},{16,24},{24,32},{32,40},{40,48},{48,56},{56,64},{64,7... | collective-permute-start | bytes 98312 | tf_op jit(solution)/shard_map/ppermute | solution.py:18
  91.8 5.4 %collective-permute-start.13 = (bf16[64,64,4]{1,0,2:T(8,128)(2,1)S(1)}, bf16[64,64,4]{1,0,2:T(8,128)(2,1)}, u32[]{:S(2)}, u32[]{:S(2)}) collective-permute-start(bf16[64,64,4]{1,0,2:T(8,128)(2,1)S(1)} %copy.42), channel_id=1, source_target_pairs={{8,0},{16,8},{24,16},{32,24},{40,32},{48,40},{56,48},{64,56},{72,6... | collective-permute-start | bytes 98312 | tf_op jit(solution)/shard_map/ppermute | solution.py:21
  99.0 6.3 %collective-permute-start.14 = (bf16[64,4,136]{2,1,0:T(4,128)(2,1)S(1)}, bf16[64,4,136]{2,1,0:T(4,128)(2,1)S(1)}, u32[]{:S(2)}, u32[]{:S(2)}) collective-permute-start(bf16[64,4,136]{2,1,0:T(4,128)(2,1)S(1)} %get-tuple-element.5), channel_id=1, source_target_pairs={{0,1},{1,2},{2,3},{3,4},{4,5},{5,6},{6,7},{8,9},{9,10},{10,11},{11... | collective-permute-start | bytes 208904 | tf_op jit(solution)/shard_map/ppermute | solution.py:18
  102.2 9.1 %collective-permute-start.15 = (bf16[64,4,136]{2,1,0:T(4,128)(2,1)S(1)}, bf16[64,4,136]{2,1,0:T(4,128)(2,1)S(1)}, u32[]{:S(2)}, u32[]{:S(2)}) collective-permute-start(bf16[64,4,136]{2,1,0:T(4,128)(2,1)S(1)} %get-tuple-element.4), channel_id=1, source_target_pairs={{1,0},{2,1},{3,2},{4,3},{5,4},{6,5},{7,6},{9,8},{10,9},{11,10},{12... | collective-permute-start | bytes 208904 | tf_op jit(solution)/shard_map/ppermute | solution.py:21
  118.7 1.2 copy-start.6
  124.0 1.2 copy-start.4
  124.0 1.2 copy-start.12
  125.0 96.4 %copy-start.1 = (bf16[256,128]{1,0:T(8,128)(2,1)S(1)}, bf16[256,128]{1,0:T(8,128)(2,1)}, u32[]{:S(2)}) copy-start(bf16[256,128]{1,0:T(8,128)(2,1)} %param.12) | copy-start | bytes 196612
  125.2 2.9 %copy-start.9 = (f32[64,128]{1,0:T(8,128)S(1)}, f32[64,128]{1,0:T(8,128)}, u32[]{:S(2)}) copy-start(f32[64,128]{1,0:T(8,128)} %param.16) | copy-start | bytes 98308
  125.2 2.9 %copy-start.10 = (s32[64,128]{1,0:T(8,128)S(1)}, s32[64,128]{1,0:T(8,128)}, u32[]{:S(2)}) copy-start(s32[64,128]{1,0:T(8,128)} %param.17) | copy-start | bytes 98308
  128.1 93.2 %copy-start.7 = (f32[8192]{0:T(1024)}, f32[8192]{0:T(1024)S(1)}, u32[]{:S(2)}) copy-start(f32[8192]{0:T(1024)S(1)} %fusion.5) | copy-start | bytes 98308
where the time goes:
time: 224 us; the launch traced here: 222 us
  blocking collectives  91.9 us (41%)
  starting transfers between devices  41.4 us (18%)
  waiting for transfers between devices  28.2 us (13%)
  local copies, waits for them, and re-layouts  25.7 us (11%)
  matrix products  20.6 us (9%)
  other arithmetic  11.7 us (5%)
  between operations  3.09 us (1%)
    psum x1, blocking collectives, body(): summed = lax.psum(partial_err, ('diag', 'off'))  91.9 us
    ppermute x6, starting transfers between devices, with_halo(): lax.ppermute(lax.slice_in_dim(block, block.shape[dim] - width, None, axis...  27 us
    ppermute x6, waiting for transfers between devices, with_halo(): lax.ppermute(lax.slice_in_dim(block, 0, width, axis=dim), axis, backward)  16.3 us
    dot_general x18, matrix products, filter_taps(): jnp.dot(weight[tap_off, tap_bin], piece, preferred_element_type=jnp.float32)  14.2 us
    ppermute x4, waiting for transfers between devices, passed_along(): return lax.ppermute(block, axis, route)  11.9 us
    unnamed x96, local copies, waits for them, and re-layouts  11.4 us
    ppermute x6, starting transfers between devices, with_halo(): lax.ppermute(lax.slice_in_dim(block, 0, width, axis=dim), axis, backward)  9.19 us
    concatenate x5, other arithmetic, with_halo(): block = jnp.concatenate([low, block, high], axis=dim)  8.2 us
  transfers between devices with their start and end apart: 16, of which 7 were waited for; matrix products, arithmetic and copies ran while one was open for 5% of the time, Pallas kernels for 0%

commit v1 on v0

v1 whole, which is shorter than its diff:
```python
import functools

import jax
import jax.numpy as jnp
import ml_dtypes
import numpy as np
from jax import lax
from jax.experimental import pallas as pl
from jax.experimental.pallas import tpu as pltpu
from jax.sharding import PartitionSpec as P

BINS = 4096
BAND = 512
CP = 64
D = 256
N_DIAG = 32
N_OFF = 8
W_LEFT = 192
W_RIGHT = 256
ROWS = W_LEFT + W_RIGHT
F32 = jnp.float32
BF16 = jnp.bfloat16
NT = (((1,), (1,)), ((), ()))


def selections():
    def one_hot(index, width):
        index = np.asarray(index).reshape(-1)
        return (index[:, None] == np.arange(width)[None, :]).astype(ml_dtypes.bfloat16)

    par, v, r, s = np.meshgrid(np.arange(2), np.arange(27), np.arange(4), np.arange(4), indexing="ij")
    right = one_hot(4 * (2 * v + par) + r + s + 16, W_RIGHT)
    par, jj, r, s = np.meshgrid(np.arange(2), np.arange(18), np.arange(4), np.arange(4), indexing="ij")
    left = one_hot(4 * (2 * jj + par) + s + 24, W_LEFT)
    m, r, s = np.meshgrid(np.arange(10), np.arange(4), np.arange(4), indexing="ij")
    embed = one_hot(8 * m + r + 8, 96)
    jo, jj, r, s = np.meshgrid(np.arange(2), np.arange(16), np.arange(4), np.arange(4), indexing="ij")
    back = one_hot(r * 128 + 4 * (2 * jj + jo) + s, 512)
    return right, left, embed, back


def dot(a, b):
    return jnp.dot(a, b, preferred_element_type=F32)


def dot_nt(a, b):
    return lax.dot_general(a, b, NT, preferred_element_type=F32)


def kernel(
    feat, conv, outw, proj, emb, filt, head, target, mask, sel_r, sel_l, sel_e, sel_b,
    pred, loss,
    win, ewin, wconv, wout, wproj, wfilt, vtarget, vmask, vsel_r, vsel_l, vsel_e, vsel_b,
    first, gin, gpair, rr, ll, ee, pair, inner, red1, red2,
    local_sem, send_sem, recv_sem, self_sem, s1, r1, s2, r2,
):
    d = lax.axis_index("diag")
    g = lax.axis_index("off")
    h = g // 2
    odd = g % 2

    left_moves = [(0, -1, 96, 32, 0), (1, 1, 0, 32, 160)]
    even_moves = [(2, h - 1, 96, 32, 192), (3, h, 0, 128, 224), (4, h + 1, 0, 96, 352)]
    odd_moves = [(2, h, 32, 96, 192), (3, h + 1, 0, 128, 288), (4, h + 2, 0, 32, 416)]
    embed_moves = [(5, -1, 48, 0), (6, 1, 0, 80)]

    def sends_to(ahead):
        return jnp.logical_and(d - ahead >= 0, d - ahead < N_DIAG)

    def hears_from(ahead):
        return jnp.logical_and(d + ahead >= 0, d + ahead < N_DIAG)

    def move(number, ahead, start, count, to):
        return pltpu.make_async_remote_copy(
            src_ref=feat.at[pl.ds(start, count)],
            dst_ref=win.at[pl.ds(to, count)],
            send_sem=send_sem.at[number],
            recv_sem=recv_sem.at[number],
            device_id=(d - ahead, g),
            device_id_type=pl.DeviceIdType.MESH,
        )

    def own_move(start, count, to):
        return pltpu.make_async_copy(feat.at[pl.ds(start, count)], win.at[pl.ds(to, count)], self_sem)

    def embed_move(number, ahead, start, to):
        return pltpu.make_async_remote_copy(
            src_ref=emb.at[pl.ds(start, 16)],
            dst_ref=ewin.at[pl.ds(to, 16)],
            send_sem=send_sem.at[number],
            recv_sem=recv_sem.at[number],
            device_id=(d, g - ahead),
            device_id_type=pl.DeviceIdType.MESH,
        )

    barrier = pltpu.get_barrier_semaphore()

    def greet(peer_d, peer_g):
        pl.semaphore_signal(barrier, inc=1, device_id=(peer_d, peer_g), device_id_type=pl.DeviceIdType.MESH)

    def away(ahead):
        return ahead != 0 if not isinstance(ahead, int) else True

    def count_of(cond):
        return jnp.where(cond, 1, 0).astype(jnp.int32)

    total = jnp.int32(30)
    for reach in (-1, 1):
        ok_s = jnp.logical_and(d - reach >= 0, d - reach < N_DIAG)

        @pl.when(ok_s)
        def _(reach=reach):
            greet(d - reach, g)
            greet(d - reach, g)

        total = total + 2 * count_of(ok_s)
        ok_g = jnp.logical_and(g - reach >= 0, g - reach < N_OFF)

        @pl.when(ok_g)
        def _(reach=reach):
            greet(d, g - reach)
            greet(d, g - reach)

        total = total + 2 * count_of(ok_g)
    for step in range(3):
        ahead = h - 1 + odd + step
        ok_s = jnp.logical_and(sends_to(ahead), ahead != 0)
        ok_r = jnp.logical_and(hears_from(ahead), ahead != 0)

        @pl.when(ok_s)
        def _(ahead=ahead):
            greet(d - ahead, g)

        @pl.when(ok_r)
        def _(ahead=ahead):
            greet(d + ahead, g)

        total = total + count_of(ok_s) + count_of(ok_r)

    t1 = (d // 16) * 8 + g
    t2 = d % 16

    def peer1(k):
        t = (t1 + k) % 16
        return t, ((t // 8) * 16 + t2, t % 8)

    def peer2(k):
        t = (t2 + k) % 16
        return t, ((d // 16) * 16 + t, g)

    def greet_both(k, carry):
        greet(*peer1(k)[1])
        greet(*peer2(k)[1])
        return carry

    lax.fori_loop(1, 16, greet_both, 0)

    loads = [(feat, win.at[pl.ds(32, 128)])]
    loads += [(emb, ewin.at[pl.ds(16, 64)])]
    loads += [(filt, wfilt)]
    for layer in range(2):
        for tap in range(3):
            loads.append((conv.at[layer, tap], wconv.at[layer, :, pl.ds(128 * tap, 128)]))
    loads += [(outw, wout), (proj, wproj), (sel_r, vsel_r), (sel_l, vsel_l), (sel_e, vsel_e), (sel_b, vsel_b)]
    loads += [(target, vtarget), (mask, vmask)]
    copies = [pltpu.make_async_copy(a, b, local_sem.at[i]) for i, (a, b) in enumerate(loads)]
    for copy in copies:
        copy.start()

    pl.semaphore_wait(barrier, total)

    def run_moves(moves, act):
        for number, ahead, start, count, to in moves:
            act(number, ahead, start, count, to)

    def begin(number, ahead, start, count, to):
        if isinstance(ahead, int):
            pl.when(sends_to(ahead))(lambda: move(number, ahead, start, count, to).start())
            return
        pl.when(jnp.logical_and(sends_to(ahead), ahead != 0))(
            lambda: move(number, ahead, start, count, to).start()
        )
        pl.when(ahead == 0)(lambda: own_move(start, count, to).start())

    def finish(number, ahead, start, count, to):
        if isinstance(ahead, int):
            pl.when(hears_from(ahead))(lambda: move(number, ahead, start, count, to).wait_recv())
            return
        pl.when(jnp.logical_and(hears_from(ahead), ahead != 0))(
            lambda: move(number, ahead, start, count, to).wait_recv()
        )
        pl.when(ahead == 0)(lambda: own_move(start, count, to).wait())

    def retire(number, ahead, start, count, to):
        if isinstance(ahead, int):
            pl.when(sends_to(ahead))(lambda: move(number, ahead, start, count, to).wait_send())
            return
        pl.when(jnp.logical_and(sends_to(ahead), ahead != 0))(
            lambda: move(number, ahead, start, count, to).wait_send()
        )

    def all_moves(act):
        @pl.when(odd == 0)
        def _():
            run_moves(even_moves, act)

        @pl.when(odd == 1)
        def _():
            run_moves(odd_moves, act)

        run_moves(left_moves, act)

    all_moves(begin)
    for number, ahead, start, to in embed_moves:
        ok = jnp.logical_and(g - ahead >= 0, g - ahead < N_OFF)
        pl.when(ok)(lambda n=number, a=ahead, s=start, t=to: embed_move(n, a, s, t).start())

    copies[2].wait()
    lane = lax.broadcasted_iota(jnp.int32, (64, 128), 1)
    row64 = lax.broadcasted_iota(jnp.int32, (64, 128), 0)
    twice = jnp.where(lane % 64 == row64, 1.0, 0.0).astype(BF16)
    low = lane < 64
    taps = dot(wfilt[...], twice)

    def tap_of(layer, p, q):
        start = ((layer * 3 + p) * 3 + q) * 64
        return taps[start : start + 64]

    none = jnp.zeros((64, 128), F32)
    for jin in range(4):
        for jout in range(2):
            for kout in range(2):
                q = jin - jout
                base = (jout * 2 + kout) * 64
                rows = pl.ds(base, 64)
                if q < 0 or q > 2:
                    halves = (none, none)
                elif kout == 0:
                    halves = (jnp.where(low, tap_of(0, 0, q), tap_of(0, 1, q)), jnp.where(low, tap_of(0, 2, q), none))
                else:
                    halves = (jnp.where(low, none, tap_of(0, 0, q)), jnp.where(low, tap_of(0, 1, q), tap_of(0, 2, q)))
                first[jin, rows, 0:128] = halves[0].astype(BF16)
                first[jin, rows, 128:256] = halves[1].astype(BF16)

    head_row = head[0:1, :]
    h0 = head_row.astype(BF16).astype(F32)
    h1 = (head_row - h0).astype(BF16).astype(F32)
    h2 = (head_row - h0 - h1).astype(BF16).astype(F32)
    row8 = lax.broadcasted_iota(jnp.int32, (8, 64), 0)
    head8 = jnp.where(row8 == 0, h0, jnp.where(row8 == 1, h1, jnp.where(row8 == 2, h2, 0.0))).astype(BF16)
    head_twice = jnp.sum(dot(head8, twice), axis=0, keepdims=True)
    row96 = lax.broadcasted_iota(jnp.int32, (96, 128), 0)
    lane96 = lax.broadcasted_iota(jnp.int32, (96, 128), 1)
    k_out = row96 % 16
    kp = lane96 // 64
    q_of = row96 // 32

    def hi_lo(value):
        hi = value.astype(BF16).astype(F32)
        return hi, (value - hi).astype(BF16).astype(F32)

    folded = []
    for p in range(3):
        pieces = []
        for q in range(3):
            whole = jnp.sum(dot(head8, tap_of(1, p, q).astype(BF16)), axis=0, keepdims=True)
            for part in hi_lo(whole):
                pieces.append(jnp.broadcast_to(part, (16, 128)))
        folded.append(jnp.concatenate(pieces, axis=0))
    for m in range(9):
        p_of = 2 * m + kp - k_out
        block = jnp.zeros((96, 128), F32)
        for p in range(3):
            block = jnp.where(p_of == p, folded[p], block)
        gin[:, m * 128 : (m + 1) * 128] = block.astype(BF16)
    head_hi, head_lo = hi_lo(head_twice)
    head_block = jnp.where(row96 % 32 < 16, head_hi, head_lo)
    for m in range(8):
        block = jnp.where(jnp.logical_and(q_of == 1, 2 * m + kp == k_out), head_block, 0.0)
        gpair[:, m * 128 : (m + 1) * 128] = block.astype(BF16)

    for copy in copies[:2] + copies[3:]:
        copy.wait()
    for number, ahead, start, to in embed_moves:
        ok = jnp.logical_and(g + ahead >= 0, g + ahead < N_OFF)
        pl.when(ok)(lambda n=number, a=ahead, s=start, t=to: embed_move(n, a, s, t).wait_recv())
    erow = lax.broadcasted_iota(jnp.int32, (96, 64), 0) + 64 * g - 16
    e_in = jnp.logical_and(erow >= 0, erow < BAND)
    e_val = jnp.where(e_in, ewin[...].astype(F32), 0.0).astype(BF16)
    e_two = dot(e_val, twice)
    e_two = jnp.where(lane96 < 64, e_two, pltpu.roll(e_two, 92, 0)).astype(BF16)
    ee[...] = dot(vsel_e[...], e_two).reshape(10, 16, 128)

    all_moves(finish)
    row = lax.broadcasted_iota(jnp.int32, (ROWS, 1), 0)
    bin_of = 128 * d - 32 + jnp.where(row < W_LEFT, row, row - W_LEFT + 64 * g)
    inside = jnp.logical_and(bin_of >= 0, bin_of < BINS)
    x = jnp.where(inside, win[...].astype(F32), 0.0)
    for layer, spread in ((0, 4), (1, 8)):
        y = dot(jnp.maximum(x, 0.0).astype(BF16), wconv[layer])
        c = pltpu.roll(y[:, 0:128], spread, 0) + y[:, 128:256] + pltpu.roll(y[:, 256:384], ROWS - spread, 0)
        v = jnp.maximum(c, 0.0).astype(BF16)
        x = jnp.where(inside, (x + dot(v, wout[layer])).astype(BF16).astype(F32), 0.0)
    projected = dot(x.astype(BF16), wproj[...]).astype(BF16).astype(F32)
    projected = jnp.where(inside, projected, 0.0)
    swapped = pltpu.roll(projected, 64, 1)
    lane_r = lax.broadcasted_iota(jnp.int32, (W_RIGHT, 128), 1) < 64
    lane_l = lax.broadcasted_iota(jnp.int32, (W_LEFT, 128), 1) < 64
    left = jnp.where(lane_l, projected[:W_LEFT], swapped[:W_LEFT]).astype(BF16)
    ahead4 = pltpu.roll(projected[W_LEFT:], W_RIGHT - 4, 0)
    right = jnp.where(lane_r, swapped[W_LEFT:], ahead4).astype(BF16)
    ll[...] = dot(vsel_l[...], left).reshape(2, 288, 128)
    rr[...] = dot(vsel_r[...], right).reshape(2, 432, 128)

    def build(m, carry):
        e = jnp.broadcast_to(ee[m][None], (18, 16, 128)).reshape(288, 128)
        for par in range(2):
            value = rr[par, pl.ds(pl.multiple_of(m * 16, 16), 288), :] + ll[par] + e
            pair[par, :, pl.ds(pl.multiple_of(m * 128, 128), 128)] = jnp.maximum(value, 0.0).astype(BF16)
        return carry

    lax.fori_loop(0, 10, build, 0)

    @pl.when(d == 0)
    def _():
        pair[:, 0:16, :] = jnp.zeros((2, 16, 1280), BF16)

    @pl.when(d == N_DIAG - 1)
    def _():
        pair[:, 272:288, :] = jnp.zeros((2, 16, 1280), BF16)

    @pl.when(g == 0)
    def _():
        pair[:, :, 0:128] = jnp.zeros((2, 288, 128), BF16)

    @pl.when(g == N_OFF - 1)
    def _():
        pair[:, :, 1152:1280] = jnp.zeros((2, 288, 128), BF16)

    def convolve(m, carry):
        cols = pl.ds(pl.multiple_of(m * 128, 128), 256)
        acc = dot_nt(pair[0, 0:272, cols], first[0])
        acc = acc + dot_nt(pair[1, 0:272, cols], first[1])
        acc = acc + dot_nt(pair[0, 16:288, cols], first[2])
        acc = acc + dot_nt(pair[1, 16:288, cols], first[3])
        acc = jnp.maximum(acc, 0.0).astype(BF16)
        out_cols = pl.ds(pl.multiple_of(m * 128, 128), 128)
        inner[0, :, out_cols] = acc[:, 0:128]
        inner[1, :, out_cols] = acc[:, 128:256]
        return carry

    lax.fori_loop(0, 9, convolve, 0)

    @pl.when(d == 0)
    def _():
        inner[0, 0:16, :] = jnp.zeros((16, 1152), BF16)

    @pl.when(d == N_DIAG - 1)
    def _():
        inner[1, 256:272, :] = jnp.zeros((16, 1152), BF16)

    lane272 = lax.broadcasted_iota(jnp.int32, (272, 128), 1)

    @pl.when(g == 0)
    def _():
        for par in range(2):
            inner[par, :, 0:128] = jnp.where(lane272 < 64, 0.0, inner[par, :, 0:128].astype(F32)).astype(BF16)

    @pl.when(g == N_OFF - 1)
    def _():
        for par in range(2):
            edge = inner[par, :, 1024:1152].astype(F32)
            inner[par, :, 1024:1152] = jnp.where(lane272 < 64, edge, 0.0).astype(BF16)

    def turned(value):
        full = jnp.concatenate([value, jnp.zeros((256, 32), F32)], axis=1)
        return jnp.transpose(full)

    sums = []
    for par in range(2):
        t = dot_nt(inner[par], gin[...])
        t = t + dot_nt(pair[1 - par, 16 * par : 16 * par + 272, 128:1152], gpair[...])
        sums.append((turned(t[0:256]), turned(t[16:272])))

    def both(value, q):
        return value[32 * q : 32 * q + 16] + value[32 * q + 16 : 32 * q + 32]

    (a0, a1), (b0, b1) = sums
    even = both(a0, 0) + both(b0, 1) + both(a1, 2)
    odds = both(b0, 0) + both(a1, 1) + both(b1, 2)
    flat = jnp.concatenate([even, odds], axis=1)
    p0 = flat.astype(BF16).astype(F32)
    p1 = (flat - p0).astype(BF16).astype(F32)
    p2 = flat - p0 - p1
    stacked = jnp.concatenate([p0, p1, p2], axis=0).astype(BF16)
    placed = dot(stacked, vsel_b[...])
    placed = placed[0:16] + placed[16:32] + placed[32:48]
    for r in range(4):
        pred[pl.ds(r, 16, stride=4), :] = placed[:, r * 128 : (r + 1) * 128]

    o_of = lax.broadcasted_iota(jnp.int32, (64, 128), 0) + 64 * g
    i_of = lax.broadcasted_iota(jnp.int32, (64, 128), 1) + 128 * d
    valid = jnp.where(o_of + i_of < BINS, vmask[...].astype(F32), 0.0)
    err = valid * (pred[...] - vtarget[...]) ** 2
    red1[t1] = jnp.sum(err.reshape(8, 8, 128), axis=0)

    def reduce_copy(buf, slot, peer, send, recv, wait_slot):
        return pltpu.make_async_remote_copy(
            src_ref=buf.at[slot], dst_ref=buf.at[slot], send_sem=send, recv_sem=recv.at[wait_slot],
            device_id=peer, device_id_type=pl.DeviceIdType.MESH,
        )

    def reduce_over(buf, mine, peer, send, recv):
        def go(k, carry):
            t, where = peer(k)
            reduce_copy(buf, mine, where, send.at[k], recv, mine).start()
            return carry

        def arrived(k, carry):
            t, where = peer(k)
            reduce_copy(buf, t, where, send.at[k], recv, t).wait_recv()
            return carry

        lax.fori_loop(1, 16, go, 0)
        lax.fori_loop(1, 16, arrived, 0)
        return jnp.sum(buf[...], axis=0)

    def reduce_retire(buf, mine, peer, send, recv):
        def sent(k, carry):
            t, where = peer(k)
            reduce_copy(buf, mine, where, send.at[k], recv, mine).wait_send()
            return carry

        lax.fori_loop(1, 16, sent, 0)

    red2[t2] = reduce_over(red1, t1, peer1, s1, r1)
    total_err = reduce_over(red2, t2, peer2, s2, r2)
    loss[0, 0] = jnp.sum(total_err) / (BAND * BINS)

    all_moves(retire)
    for number, ahead, start, to in embed_moves:
        ok = jnp.logical_and(g - ahead >= 0, g - ahead < N_OFF)
        pl.when(ok)(lambda n=number, a=ahead, s=start, t=to: embed_move(n, a, s, t).wait_send())
    reduce_retire(red1, t1, peer1, s1, r1)
    reduce_retire(red2, t2, peer2, s2, r2)


def body(features, conv_weight, out_weight, proj_weight, offset_embed, pair_filter_weight, head_weight, target, cell_mask):
    anywhere = pl.BlockSpec(memory_space=pl.ANY)
    vmem = pl.BlockSpec(memory_space=pltpu.VMEM)
    picks = [jnp.asarray(value) for value in selections()]
    pred, loss = pl.pallas_call(
        kernel,
        out_shape=(jax.ShapeDtypeStruct((64, 128), F32), jax.ShapeDtypeStruct((1, 1), F32)),
        in_specs=[anywhere] * 6 + [vmem] + [anywhere] * 6,
        out_specs=(vmem, pl.BlockSpec(memory_space=pltpu.SMEM)),
        scratch_shapes=[
            pltpu.VMEM((ROWS, D), BF16),
            pltpu.VMEM((96, CP), BF16),
            pltpu.VMEM((2, D, 384), BF16),
            pltpu.VMEM((2, 128, D), BF16),
            pltpu.VMEM((D, 128), BF16),
            pltpu.VMEM((1152, CP), BF16),
            pltpu.VMEM((64, 128), F32),
            pltpu.VMEM((64, 128), jnp.int32),
            pltpu.VMEM((864, W_RIGHT), BF16),
            pltpu.VMEM((576, W_LEFT), BF16),
            pltpu.VMEM((160, 96), BF16),
            pltpu.VMEM((512, 512), BF16),
            pltpu.VMEM((4, 256, 256), BF16),
            pltpu.VMEM((96, 1152), BF16),
            pltpu.VMEM((96, 1024), BF16),
            pltpu.VMEM((2, 432, 128), F32),
            pltpu.VMEM((2, 288, 128), F32),
            pltpu.VMEM((10, 16, 128), F32),
            pltpu.VMEM((2, 288, 1280), BF16),
            pltpu.VMEM((2, 272, 1152), BF16),
            pltpu.VMEM((16, 8, 128), F32),
            pltpu.VMEM((16, 8, 128), F32),
            pltpu.SemaphoreType.DMA((17,)),
            pltpu.SemaphoreType.DMA((7,)),
            pltpu.SemaphoreType.DMA((7,)),
            pltpu.SemaphoreType.DMA,
            pltpu.SemaphoreType.DMA((16,)),
            pltpu.SemaphoreType.DMA((16,)),
            pltpu.SemaphoreType.DMA((16,)),
            pltpu.SemaphoreType.DMA((16,)),
        ],
        compiler_params=pltpu.CompilerParams(
            collective_id=0, has_side_effects=True, vmem_limit_bytes=40 * 1024 * 1024
        ),
        name="contact_block",
    )(
        features, conv_weight, out_weight, proj_weight, offset_embed,
        pair_filter_weight.reshape(1152, CP), head_weight.reshape(1, CP), target, cell_mask, *picks,
    )
    return pred, loss[0, 0]


def solution(mesh):
    in_specs = (P("diag", None), P(), P(), P(), P("off", None), P(), P(), P("off", "diag"), P("off", "diag"))
    out_specs = (P("off", "diag"), P())
    return jax.shard_map(body, mesh=mesh, in_specs=in_specs, out_specs=out_specs, check_vma=False)
```

time: 224 us -> 49.5 us (0.22)
  blocking collectives: 91.9 us -> 0 us
  starting transfers between devices: 41.4 us -> 0 us
  Pallas kernels: 0 us -> 34.6 us
  waiting for transfers between devices: 28.2 us -> 0 us
  matrix products: 20.6 us -> 0 us
  local copies, waits for them, and re-layouts: 25.7 us -> 11.8 us
  other arithmetic: 11.7 us -> 0 us
    psum x1 -> x0, blocking collectives: 91.9 us -> none  [body(): summed = lax.psum(partial_err, ('diag', 'off'))]
    ppermute x16 -> x0, starting transfers between devices: 41.4 us -> none  [the longest x6 27 us: with_halo(): lax.ppermute(lax.slice_in_dim(block, block.shape[dim] - width, None, axis...]
    pallas_call x0 -> x1, Pallas kernels: none -> 34.6 us  [body(): pl.pallas_call(kernel, out_shape=(jax.ShapeDtypeStruct((64, 128), F32), j...]
    ppermute x16 -> x0, waiting for transfers between devices: 28.2 us -> none  [the longest x6 16.3 us: with_halo(): lax.ppermute(lax.slice_in_dim(block, 0, width, axis=dim), axis, backward)]
    dot_general x25 -> x0, matrix products: 20.6 us -> none  [the longest x18 14.2 us: filter_taps(): jnp.dot(weight[tap_off, tap_bin], piece, preferred_element_type=jnp.float32)]
    concatenate x5 -> x0, other arithmetic: 8.2 us -> none  [with_halo(): block = jnp.concatenate([low, block, high], axis=dim)]
    slice x8 -> x0, local copies, waits for them, and re-layouts: 6.72 us -> none  [the longest x5 2.86 us: with_halo(): lax.slice_in_dim(block, block.shape[dim] - width, None, axis=dim)]
    ppermute x4 -> x0, local copies, waits for them, and re-layouts: 6.34 us -> none  [the longest x2 4 us: with_halo(): lax.ppermute(lax.slice_in_dim(block, 0, width, axis=dim), axis, backward)]
  transfers between devices with their start and end apart: 16 -> 0, of which waited for: 7 -> 0; matrix products, arithmetic and copies ran while one was open for 5% -> 0% of each run, Pallas kernels for 0% -> 0%
where the time goes in v1:
time: 49.5 us; the launch traced here: 48.8 us
  Pallas kernels  34.6 us (70%)
  local copies, waits for them, and re-layouts  11.8 us (24%)
  between operations  2.35 us (5%)
    pallas_call x1, Pallas kernels, body(): pl.pallas_call(kernel, out_shape=(jax.ShapeDtypeStruct((64, 128), F32), j...  34.6 us
    unnamed x27, local copies, waits for them, and re-layouts  11.8 us

profile of v1, /device:TPU:1, one launch (start us, length us, event | category | flops | bytes accessed | tf_op | source)
XLA Modules:
  0.0 48.8 jit_solution(10508786854914646560)
XLA Ops:
  0.6 0.0 copy-start.12
  0.6 0.6 %copy-done.12 = f32[64]{0:T(128)S(1)} copy-done((f32[64]{0:T(128)S(1)}, f32[64]{0:T(128)}, u32[]{:S(2)}) %copy-start.12) | copy-done | bytes 280
  1.3 0.0 copy-start
  1.3 1.0 %copy-done = bf16[512,512]{1,0:T(8,128)(2,1)S(1)} copy-done((bf16[512,512]{1,0:T(8,128)(2,1)S(1)}, bf16[512,512]{1,0:T(8,128)(2,1)}, u32[]{:S(2)}) %copy-start) | copy-done | bytes 524312
  2.3 0.0 copy-start.1
  2.3 1.0 %copy-done.1 = bf16[864,256]{1,0:T(8,128)(2,1)S(1)} copy-done((bf16[864,256]{1,0:T(8,128)(2,1)S(1)}, bf16[864,256]{1,0:T(8,128)(2,1)}, u32[]{:S(2)}) %copy-start.1) | copy-done | bytes 442392
  3.3 0.0 copy-start.2
  3.3 1.0 %copy-done.2 = bf16[2,3,256,128]{3,2,1,0:T(8,128)(2,1)S(1)} copy-done((bf16[2,3,256,128]{3,2,1,0:T(8,128)(2,1)S(1)}, bf16[2,3,256,128]{3,2,1,0:T(8,128)(2,1)}, u32[]{:S(2)}) %copy-start.2) | copy-done | bytes 393240
  4.3 0.0 copy-start.3
  4.3 1.0 %copy-done.3 = bf16[2,3,3,64,64]{4,3,2,1,0:T(8,128)(2,1)S(1)} copy-done((bf16[2,3,3,64,64]{4,3,2,1,0:T(8,128)(2,1)S(1)}, bf16[2,3,3,64,64]{4,3,2,1,0:T(8,128)(2,1)}, u32[]{:S(2)}) %copy-start.3) | copy-done | bytes 147480
  5.3 0.0 copy-start.4
  5.3 1.0 %copy-done.4 = bf16[576,192]{1,0:T(8,128)(2,1)S(1)} copy-done((bf16[576,192]{1,0:T(8,128)(2,1)S(1)}, bf16[576,192]{1,0:T(8,128)(2,1)}, u32[]{:S(2)}) %copy-start.4) | copy-done | bytes 221208
  6.3 0.0 copy-start.5
  6.3 0.9 %copy-done.5 = bf16[2,128,256]{2,1,0:T(8,128)(2,1)S(1)} copy-done((bf16[2,128,256]{2,1,0:T(8,128)(2,1)S(1)}, bf16[2,128,256]{2,1,0:T(8,128)(2,1)}, u32[]{:S(2)}) %copy-start.5) | copy-done | bytes 131096
  7.2 0.0 copy-start.6
  7.2 0.8 %copy-done.6 = bf16[128,256]{1,0:T(8,128)(2,1)S(1)} copy-done((bf16[128,256]{1,0:T(8,128)(2,1)S(1)}, bf16[128,256]{1,0:T(8,128)(2,1)}, u32[]{:S(2)}) %copy-start.6) | copy-done | bytes 65560
  8.0 0.0 copy-start.7
  8.0 0.8 %copy-done.7 = bf16[256,128]{1,0:T(8,128)(2,1)S(1)} copy-done((bf16[256,128]{1,0:T(8,128)(2,1)S(1)}, bf16[256,128]{1,0:T(8,128)(2,1)}, u32[]{:S(2)}) %copy-start.7) | copy-done | bytes 65560
  8.8 0.0 copy-start.8
  8.9 0.8 %copy-done.8 = bf16[160,96]{1,0:T(8,128)(2,1)S(1)} copy-done((bf16[160,96]{1,0:T(8,128)(2,1)S(1)}, bf16[160,96]{1,0:T(8,128)(2,1)}, u32[]{:S(2)}) %copy-start.8) | copy-done | bytes 30744
  9.6 0.0 copy-start.9
  9.6 0.8 %copy-done.9 = f32[64,128]{1,0:T(8,128)S(1)} copy-done((f32[64,128]{1,0:T(8,128)S(1)}, f32[64,128]{1,0:T(8,128)}, u32[]{:S(2)}) %copy-start.9) | copy-done | bytes 32792
  10.4 0.0 copy-start.10
  10.4 0.8 %copy-done.10 = s32[64,128]{1,0:T(8,128)S(1)} copy-done((s32[64,128]{1,0:T(8,128)S(1)}, s32[64,128]{1,0:T(8,128)}, u32[]{:S(2)}) %copy-start.10) | copy-done | bytes 32792
  11.1 0.0 copy-start.11
  11.1 0.7 %copy-done.11 = bf16[64,64]{1,0:T(8,128)(2,1)S(1)} copy-done((bf16[64,64]{1,0:T(8,128)(2,1)S(1)}, bf16[64,64]{1,0:T(8,128)(2,1)}, u32[]{:S(2)}) %copy-start.11) | copy-done | bytes 8216
  11.9 34.6 %contact_block.1 = (f32[64,128]{1,0:T(8,128)S(1)}, f32[1,1]{1,0:T(1,128)}) custom-call(bf16[128,256]{1,0:T(8,128)(2,1)S(1)} %copy-done.6, bf16[2,3,256,128]{3,2,1,0:T(8,128)(2,1)S(1)} %copy-done.2, bf16[2,128,256]{2,1,0:T(8,128)(2,1)S(1)} %copy-done.5, bf16[256,128]{1,0:T(8,128)(2,1)S(1)} %copy-done.7, bf16[64,64]{1,0:T(8,128)(2,1)S(1)} %copy-done.11, ...), custom_call_target="tpu_custom_call" | custom-call | tf_op jit(solution)/shard_map/contact_block/pallas_call | solution.py:452
  46.5 0.6 %copy.17 = f32[64,128]{1,0:T(8,128)} copy(f32[64,128]{1,0:T(8,128)S(1)} %get-tuple-element.8) | data formatting | bytes 65536
Async XLA Ops:
  0.6 0.7 %copy-start.12 = (f32[64]{0:T(128)S(1)}, f32[64]{0:T(128)}, u32[]{:S(2)}) copy-start(f32[64]{0:T(128)} %param.19) | copy-start | bytes 772
  1.3 1.0 %copy-start = (bf16[512,512]{1,0:T(8,128)(2,1)S(1)}, bf16[512,512]{1,0:T(8,128)(2,1)}, u32[]{:S(2)}) copy-start(bf16[512,512]{1,0:T(8,128)(2,1)} %constant.11.clone.sel_b) | copy-start | bytes 1572868
  2.3 1.0 %copy-start.1 = (bf16[864,256]{1,0:T(8,128)(2,1)S(1)}, bf16[864,256]{1,0:T(8,128)(2,1)}, u32[]{:S(2)}) copy-start(bf16[864,256]{1,0:T(8,128)(2,1)} %constant.8.clone.sel_r) | copy-start | bytes 1327108
  3.3 1.0 %copy-start.2 = (bf16[2,3,256,128]{3,2,1,0:T(8,128)(2,1)S(1)}, bf16[2,3,256,128]{3,2,1,0:T(8,128)(2,1)}, u32[]{:S(2)}) copy-start(bf16[2,3,256,128]{3,2,1,0:T(8,128)(2,1)} %conv.1) | copy-start | bytes 1179652
  4.3 1.0 %copy-start.3 = (bf16[2,3,3,64,64]{4,3,2,1,0:T(8,128)(2,1)S(1)}, bf16[2,3,3,64,64]{4,3,2,1,0:T(8,128)(2,1)}, u32[]{:S(2)}) copy-start(bf16[2,3,3,64,64]{4,3,2,1,0:T(8,128)(2,1)} %param.18) | copy-start | bytes 442372
  5.3 1.0 %copy-start.4 = (bf16[576,192]{1,0:T(8,128)(2,1)S(1)}, bf16[576,192]{1,0:T(8,128)(2,1)}, u32[]{:S(2)}) copy-start(bf16[576,192]{1,0:T(8,128)(2,1)} %constant.9.clone.sel_l) | copy-start | bytes 663556
  6.3 0.9 %copy-start.5 = (bf16[2,128,256]{2,1,0:T(8,128)(2,1)S(1)}, bf16[2,128,256]{2,1,0:T(8,128)(2,1)}, u32[]{:S(2)}) copy-start(bf16[2,128,256]{2,1,0:T(8,128)(2,1)} %outw.1) | copy-start | bytes 393220
  7.2 0.8 %copy-start.6 = (bf16[128,256]{1,0:T(8,128)(2,1)S(1)}, bf16[128,256]{1,0:T(8,128)(2,1)}, u32[]{:S(2)}) copy-start(bf16[128,256]{1,0:T(8,128)(2,1)} %feat.1) | copy-start | bytes 196612
  8.0 0.8 %copy-start.7 = (bf16[256,128]{1,0:T(8,128)(2,1)S(1)}, bf16[256,128]{1,0:T(8,128)(2,1)}, u32[]{:S(2)}) copy-start(bf16[256,128]{1,0:T(8,128)(2,1)} %proj.1) | copy-start | bytes 196612
  8.8 0.8 %copy-start.8 = (bf16[160,96]{1,0:T(8,128)(2,1)S(1)}, bf16[160,96]{1,0:T(8,128)(2,1)}, u32[]{:S(2)}) copy-start(bf16[160,96]{1,0:T(8,128)(2,1)} %constant.10.clone.sel_e) | copy-start | bytes 92164
  9.6 0.8 %copy-start.9 = (f32[64,128]{1,0:T(8,128)S(1)}, f32[64,128]{1,0:T(8,128)}, u32[]{:S(2)}) copy-start(f32[64,128]{1,0:T(8,128)} %target.1) | copy-start | bytes 98308
  10.4 0.8 %copy-start.10 = (s32[64,128]{1,0:T(8,128)S(1)}, s32[64,128]{1,0:T(8,128)}, u32[]{:S(2)}) copy-start(s32[64,128]{1,0:T(8,128)} %mask.1) | copy-start | bytes 98308
  11.1 0.7 %copy-start.11 = (bf16[64,64]{1,0:T(8,128)(2,1)S(1)}, bf16[64,64]{1,0:T(8,128)(2,1)}, u32[]{:S(2)}) copy-start(bf16[64,64]{1,0:T(8,128)(2,1)} %emb.1) | copy-start | bytes 24580

commit v2 on v1

v2 whole, which is shorter than its diff:
```python
import jax
import jax.numpy as jnp
import ml_dtypes
import numpy as np
from jax import lax
from jax.experimental import pallas as pl
from jax.experimental.pallas import tpu as pltpu
from jax.sharding import PartitionSpec as P

BINS = 4096
BAND = 512
CP = 64
D = 256
N_DIAG = 32
N_OFF = 8
ROWS = 192
W_RIGHT = 256
F32 = jnp.float32
BF16 = jnp.bfloat16
NT = (((1,), (1,)), ((), ()))


def selections():
    def one_hot(index, width):
        index = np.asarray(index).reshape(-1)
        return (index[:, None] == np.arange(width)[None, :]).astype(ml_dtypes.bfloat16)

    par, v, r, s = np.meshgrid(np.arange(2), np.arange(27), np.arange(4), np.arange(4), indexing="ij")
    right = one_hot(4 * (2 * v + par) + r + s + 16, W_RIGHT)
    par, jj, r, s = np.meshgrid(np.arange(2), np.arange(18), np.arange(4), np.arange(4), indexing="ij")
    left = one_hot(4 * (2 * jj + par) + s + 24, ROWS)
    m, r, s = np.meshgrid(np.arange(10), np.arange(4), np.arange(4), indexing="ij")
    embed = one_hot(8 * m + r + 8, 96)
    jo, jj, r, s = np.meshgrid(np.arange(2), np.arange(16), np.arange(4), np.arange(4), indexing="ij")
    back = one_hot(r * 128 + 4 * (2 * jj + jo) + s, 512)
    return right, left, embed, back


def dot(a, b):
    return jnp.dot(a, b, preferred_element_type=F32)


def dot_nt(a, b):
    return lax.dot_general(a, b, NT, preferred_element_type=F32)


def kernel(
    feat, conv, outw, proj, emb, filt, head, target, mask, sel_r, sel_l, sel_e, sel_b,
    pred, loss,
    vhead, win, ewin, wconv, wout, wproj, wfilt, vtarget, vmask, vsel_r, vsel_l, vsel_e, vsel_b, vpred,
    rwin, first, gin, gpair, rr, ll, ee, pair, inner, red1, red2,
    local_sem, send_sem, recv_sem, pred_sem, s1, r1, s2, r2, vloss, loss_sem,
):
    d = lax.axis_index("diag")
    g = lax.axis_index("off")
    h = g // 2
    odd = g % 2
    core = odd
    z_lo = d // 16
    xy = d % 16
    x_at = xy // 4
    y_at = xy % 4
    z_at = 2 * h + z_lo

    feat_moves = [(0, -1, 96, 0), (1, 1, 0, 160)]
    embed_moves = [(2, -1, 48, 0), (3, 1, 0, 80)]
    even_moves = [(4, h - 1, 96, 32, 0), (5, h, 0, 128, 32), (6, h + 1, 0, 96, 160)]
    odd_moves = [(4, h, 32, 96, 0), (5, h + 1, 0, 128, 96), (6, h + 2, 0, 32, 224)]

    def on_diag(index):
        return jnp.logical_and(index >= 0, index < N_DIAG)

    def on_off(index):
        return jnp.logical_and(index >= 0, index < N_OFF)

    def remote(src, dst, number, peer):
        return pltpu.make_async_remote_copy(
            src_ref=src, dst_ref=dst, send_sem=send_sem.at[number], recv_sem=recv_sem.at[number],
            device_id=peer, device_id_type=pl.DeviceIdType.MESH,
        )

    def feat_move(number, ahead, start, to):
        return remote(win.at[pl.ds(32 + start, 32)], win.at[pl.ds(to, 32)], number, (d - ahead, g))

    def embed_move(number, ahead, start, to):
        return remote(ewin.at[pl.ds(16 + start, 16)], ewin.at[pl.ds(to, 16)], number, (d, g - ahead))

    def right_move(number, ahead, start, count, to):
        return remote(win.at[pl.ds(32 + start, count)], rwin.at[pl.ds(to, count)], number, (d - ahead, g))

    def each_right(act):
        pl.when(odd == 0)(lambda: [act(*one) for one in even_moves] and None)
        pl.when(odd == 1)(lambda: [act(*one) for one in odd_moves] and None)

    def wrapped(value, size):
        return jnp.where(value >= size, value - size, value)

    def far(step, size):
        return min(step, size - step)

    z_steps = sorted(((a, b) for a in range(8) for b in range(2) if a or b), key=lambda t: -far(t[0], 8) * 2 - t[1])
    xy_steps = sorted(((a, b) for a in range(4) for b in range(4) if a or b), key=lambda t: -far(t[0], 4) - far(t[1], 4))

    def z_peer(step):
        z = wrapped(z_at + step[0], 8)
        c = wrapped(core + step[1], 2)
        return (z % 2 * 16 + xy, z // 2 * 2 + c)

    def xy_peer(step):
        return (z_lo * 16 + wrapped(x_at + step[0], 4) * 4 + wrapped(y_at + step[1], 4), g)

    z_slot = z_at * 2 + core
    xy_slot = xy

    own = [
        pltpu.make_async_copy(feat, win.at[pl.ds(32, 128)], local_sem.at[16]),
        pltpu.make_async_copy(emb, ewin.at[pl.ds(16, 64)], local_sem.at[17]),
    ]
    for copy in own:
        copy.start()
    barrier = pltpu.get_barrier_semaphore()

    def greet(peer, times=1):
        pl.semaphore_signal(barrier, inc=times, device_id=peer, device_id_type=pl.DeviceIdType.MESH)

    def count_of(cond):
        return jnp.where(cond, 1, 0).astype(jnp.int32)

    total = jnp.int32(30)
    for reach in (-1, 1):
        ok = on_diag(d - reach)
        pl.when(ok)(lambda reach=reach: greet((d - reach, g)))
        total = total + count_of(ok)
        ok = on_off(g - reach)
        pl.when(ok)(lambda reach=reach: greet((d, g - reach)))
        total = total + count_of(ok)
    for step in range(3):
        ahead = h - 1 + odd + step
        ok_s = jnp.logical_and(on_diag(d - ahead), ahead != 0)
        ok_r = jnp.logical_and(on_diag(d + ahead), ahead != 0)
        pl.when(ok_s)(lambda ahead=ahead: greet((d - ahead, g)))
        pl.when(ok_r)(lambda ahead=ahead: greet((d + ahead, g)))
        total = total + count_of(ok_s) + count_of(ok_r)
    for step in z_steps:
        greet(z_peer(step))
    for step in xy_steps:
        greet(xy_peer(step))

    def right_begin(number, ahead, start, count, to):
        pl.when(jnp.logical_and(on_diag(d - ahead), ahead != 0))(
            lambda: right_move(number, ahead, start, count, to).start()
        )

    for copy in own:
        copy.wait()
    pl.semaphore_wait(barrier, total)
    each_right(right_begin)
    for one in feat_moves:
        pl.when(on_diag(d - one[1]))(lambda one=one: feat_move(*one).start())
    for one in embed_moves:
        pl.when(on_off(g - one[1]))(lambda one=one: embed_move(*one).start())

    loads = [(filt, wfilt), (head, vhead)]
    for layer in range(2):
        for tap in range(3):
            loads.append((conv.at[layer, tap], wconv.at[layer, :, pl.ds(128 * tap, 128)]))
    loads += [(outw, wout), (proj, wproj), (sel_l, vsel_l), (sel_e, vsel_e)]
    loads += [(sel_r, vsel_r), (sel_b, vsel_b), (target, vtarget), (mask, vmask)]
    copies = [pltpu.make_async_copy(a, b, local_sem.at[i]) for i, (a, b) in enumerate(loads)]
    for copy in copies:
        copy.start()

    copies[0].wait()
    copies[1].wait()
    lane = lax.broadcasted_iota(jnp.int32, (64, 128), 1)
    row64 = lax.broadcasted_iota(jnp.int32, (64, 128), 0)
    twice = jnp.where(lane % 64 == row64, 1.0, 0.0).astype(BF16)
    low = lane < 64
    taps = dot(wfilt[...], twice)

    def tap_of(layer, p, q):
        start = ((layer * 3 + p) * 3 + q) * 64
        return taps[start : start + 64]

    none = jnp.zeros((64, 128), F32)
    for jin in range(4):
        for jout in range(2):
            for kout in range(2):
                q = jin - jout
                base = (jout * 2 + kout) * 64
                rows = pl.ds(base, 64)
                if q < 0 or q > 2:
                    halves = (none, none)
                elif kout == 0:
                    halves = (jnp.where(low, tap_of(0, 0, q), tap_of(0, 1, q)), jnp.where(low, tap_of(0, 2, q), none))
                else:
                    halves = (jnp.where(low, none, tap_of(0, 0, q)), jnp.where(low, tap_of(0, 1, q), tap_of(0, 2, q)))
                first[rows, jin * 256 : jin * 256 + 128] = halves[0].astype(BF16)
                first[rows, jin * 256 + 128 : jin * 256 + 256] = halves[1].astype(BF16)

    head_row = vhead[0:1, :]
    h0 = head_row.astype(BF16).astype(F32)
    h1 = (head_row - h0).astype(BF16).astype(F32)
    h2 = (head_row - h0 - h1).astype(BF16).astype(F32)
    row8 = lax.broadcasted_iota(jnp.int32, (8, 64), 0)
    head8 = jnp.where(row8 == 0, h0, jnp.where(row8 == 1, h1, jnp.where(row8 == 2, h2, 0.0))).astype(BF16)
    head_twice = jnp.sum(dot(head8, twice), axis=0, keepdims=True)
    row96 = lax.broadcasted_iota(jnp.int32, (96, 128), 0)
    lane96 = lax.broadcasted_iota(jnp.int32, (96, 128), 1)
    k_out = row96 % 16
    kp = lane96 // 64
    q_of = row96 // 32

    def hi_lo(value):
        hi = value.astype(BF16).astype(F32)
        return hi, (value - hi).astype(BF16).astype(F32)

    folded = []
    for p in range(3):
        pieces = []
        for q in range(3):
            whole = jnp.sum(dot(head8, tap_of(1, p, q).astype(BF16)), axis=0, keepdims=True)
            for part in hi_lo(whole):
                pieces.append(jnp.broadcast_to(part, (16, 128)))
        folded.append(jnp.concatenate(pieces, axis=0))
    for m in range(9):
        p_of = 2 * m + kp - k_out
        block = jnp.zeros((96, 128), F32)
        for p in range(3):
            block = jnp.where(p_of == p, folded[p], block)
        gin[:, m * 128 : (m + 1) * 128] = block.astype(BF16)
    head_hi, head_lo = hi_lo(head_twice)
    head_block = jnp.where(row96 % 32 < 16, head_hi, head_lo)
    for m in range(8):
        block = jnp.where(jnp.logical_and(q_of == 1, 2 * m + kp == k_out), head_block, 0.0)
        gpair[:, m * 128 : (m + 1) * 128] = block.astype(BF16)

    for copy in copies[2:10]:
        copy.wait()
    for one in feat_moves:
        pl.when(on_diag(d + one[1]))(lambda one=one: feat_move(*one).wait_recv())

    def trunk(window, rows, start):
        at = lax.broadcasted_iota(jnp.int32, (rows, 1), 0) + start
        inside = jnp.logical_and(at >= 0, at < BINS)
        x = jnp.where(inside, window[...].astype(F32), 0.0)
        for layer, spread in ((0, 4), (1, 8)):
            y = dot(jnp.maximum(x, 0.0).astype(BF16), wconv[layer])
            c = pltpu.roll(y[:, 0:128], spread, 0) + y[:, 128:256] + pltpu.roll(y[:, 256:384], rows - spread, 0)
            v = jnp.maximum(c, 0.0).astype(BF16)
            x = jnp.where(inside, (x + dot(v, wout[layer])).astype(BF16).astype(F32), 0.0)
        value = dot(x.astype(BF16), wproj[...]).astype(BF16).astype(F32)
        return value, pltpu.roll(value, 64, 1)

    projected, swapped = trunk(win, ROWS, 128 * d - 32)

    for copy in copies[10:]:
        copy.wait()
    lane_l = lax.broadcasted_iota(jnp.int32, (ROWS, 128), 1) < 64
    left = jnp.where(lane_l, projected, swapped).astype(BF16)
    ll[...] = dot(vsel_l[...], left).reshape(2, 288, 128)
    for one in embed_moves:
        pl.when(on_off(g + one[1]))(lambda one=one: embed_move(*one).wait_recv())
    erow = lax.broadcasted_iota(jnp.int32, (96, 64), 0) + 64 * g - 16
    e_in = jnp.logical_and(erow >= 0, erow < BAND)
    e_val = jnp.where(e_in, ewin[...].astype(F32), 0.0).astype(BF16)
    e_two = dot(e_val, twice)
    e_two = jnp.where(lane96 < 64, e_two, pltpu.roll(e_two, 92, 0)).astype(BF16)
    ee[...] = dot(vsel_e[...], e_two).reshape(10, 16, 128)

    def right_finish(number, ahead, start, count, to):
        pl.when(jnp.logical_and(on_diag(d + ahead), ahead != 0))(
            lambda: right_move(number, ahead, start, count, to).wait_recv()
        )

    each_right(right_finish)

    def right_own(number, ahead, start, count, to):
        @pl.when(ahead == 0)
        def _():
            rwin[to : to + count, :] = win[32 + start : 32 + start + count, :]

    each_right(right_own)
    projected, swapped = trunk(rwin, W_RIGHT, 128 * d + 64 * g - 32)
    lane_r = lax.broadcasted_iota(jnp.int32, (W_RIGHT, 128), 1) < 64
    right = jnp.where(lane_r, swapped, pltpu.roll(projected, W_RIGHT - 4, 0)).astype(BF16)
    rr[...] = dot(vsel_r[...], right).reshape(2, 432, 128)

    for m in range(10):
        e = jnp.broadcast_to(ee[m][None], (18, 16, 128)).reshape(288, 128)
        for par in range(2):
            value = rr[par, m * 16 : m * 16 + 288, :] + ll[par] + e
            pair[par, :, m * 128 : (m + 1) * 128] = jnp.maximum(value, 0.0).astype(BF16)

    @pl.when(d == 0)
    def _():
        pair[:, 0:16, :] = jnp.zeros((2, 16, 1280), BF16)

    @pl.when(d == N_DIAG - 1)
    def _():
        pair[:, 272:288, :] = jnp.zeros((2, 16, 1280), BF16)

    @pl.when(g == 0)
    def _():
        pair[:, :, 0:128] = jnp.zeros((2, 288, 128), BF16)

    @pl.when(g == N_OFF - 1)
    def _():
        pair[:, :, 1152:1280] = jnp.zeros((2, 288, 128), BF16)

    for m in range(9):
        cols = slice(m * 128, m * 128 + 256)
        near = jnp.concatenate(
            [pair[0, 0:272, cols], pair[1, 0:272, cols], pair[0, 16:288, cols], pair[1, 16:288, cols]], axis=1
        )
        acc = jnp.maximum(dot_nt(near, first[...]), 0.0).astype(BF16)
        inner[0, :, m * 128 : (m + 1) * 128] = acc[:, 0:128]
        inner[1, :, m * 128 : (m + 1) * 128] = acc[:, 128:256]

    @pl.when(d == 0)
    def _():
        inner[0, 0:16, :] = jnp.zeros((16, 1152), BF16)

    @pl.when(d == N_DIAG - 1)
    def _():
        inner[1, 256:272, :] = jnp.zeros((16, 1152), BF16)

    lane272 = lax.broadcasted_iota(jnp.int32, (272, 128), 1)

    @pl.when(g == 0)
    def _():
        for par in range(2):
            inner[par, :, 0:128] = jnp.where(lane272 < 64, 0.0, inner[par, :, 0:128].astype(F32)).astype(BF16)

    @pl.when(g == N_OFF - 1)
    def _():
        for par in range(2):
            edge = inner[par, :, 1024:1152].astype(F32)
            inner[par, :, 1024:1152] = jnp.where(lane272 < 64, edge, 0.0).astype(BF16)

    def turned(value):
        full = jnp.concatenate([value, jnp.zeros((256, 32), F32)], axis=1)
        return jnp.transpose(full)

    sums = []
    for par in range(2):
        t = dot_nt(inner[par], gin[...])
        t = t + dot_nt(pair[1 - par, 16 * par : 16 * par + 272, 128:1152], gpair[...])
        sums.append((turned(t[0:256]), turned(t[16:272])))

    def both(value, q):
        return value[32 * q : 32 * q + 16] + value[32 * q + 16 : 32 * q + 32]

    (a0, a1), (b0, b1) = sums
    even = both(a0, 0) + both(b0, 1) + both(a1, 2)
    odds = both(b0, 0) + both(a1, 1) + both(b1, 2)
    flat = jnp.concatenate([even, odds], axis=1)
    p0 = flat.astype(BF16).astype(F32)
    p1 = (flat - p0).astype(BF16).astype(F32)
    p2 = flat - p0 - p1
    stacked = jnp.concatenate([p0, p1, p2], axis=0).astype(BF16)
    placed = dot(stacked, vsel_b[...])
    placed = placed[0:16] + placed[16:32] + placed[32:48]
    for r in range(4):
        vpred[pl.ds(r, 16, stride=4), :] = placed[:, r * 128 : (r + 1) * 128]
    out_copy = pltpu.make_async_copy(vpred, pred, pred_sem)
    out_copy.start()

    o_of = lax.broadcasted_iota(jnp.int32, (64, 128), 0) + 64 * g
    i_of = lax.broadcasted_iota(jnp.int32, (64, 128), 1) + 128 * d
    valid = jnp.where(o_of + i_of < BINS, vmask[...].astype(F32), 0.0)
    err = valid * (vpred[...] - vtarget[...]) ** 2

    def reduce_over(buf, slot, value, steps, peer, send, recv):
        buf[slot] = value
        for step in steps:
            pltpu.make_async_remote_copy(
                src_ref=buf.at[slot], dst_ref=buf.at[slot], send_sem=send, recv_sem=recv,
                device_id=peer(step), device_id_type=pl.DeviceIdType.MESH,
            ).start()
        pltpu.make_async_copy(buf.at[pl.ds(0, 15)], buf.at[pl.ds(0, 15)], recv).wait()
        return jnp.sum(buf[...], axis=0)

    def reduce_retire(buf, send):
        pltpu.make_async_copy(buf.at[pl.ds(0, 15)], buf.at[pl.ds(0, 15)], send).wait()

    partial = jnp.sum(err.reshape(8, 8, 128), axis=0)
    partial = reduce_over(red1, z_slot, partial, z_steps, z_peer, s1, r1)
    partial = reduce_over(red2, xy_slot, partial, xy_steps, xy_peer, s2, r2)
    vloss[...] = partial
    loss_copy = pltpu.make_async_copy(vloss, loss, loss_sem)
    loss_copy.start()

    out_copy.wait()
    loss_copy.wait()
    for one in feat_moves:
        pl.when(on_diag(d - one[1]))(lambda one=one: feat_move(*one).wait_send())
    for one in embed_moves:
        pl.when(on_off(g - one[1]))(lambda one=one: embed_move(*one).wait_send())

    def right_retire(number, ahead, start, count, to):
        pl.when(jnp.logical_and(on_diag(d - ahead), ahead != 0))(
            lambda: right_move(number, ahead, start, count, to).wait_send()
        )

    each_right(right_retire)
    reduce_retire(red1, s1)
    reduce_retire(red2, s2)


def finish(pred_in, parts, pred, loss):
    pred[...] = pred_in[...]
    loss[0, 0] = jnp.sum(parts[...]) / (BAND * BINS)


def body(features, conv_weight, out_weight, proj_weight, offset_embed, pair_filter_weight, head_weight, target, cell_mask):
    vmem = pl.BlockSpec(memory_space=pltpu.VMEM)
    anywhere = pl.BlockSpec(memory_space=pltpu.HBM)
    picks = [jnp.asarray(value) for value in selections()]
    pred, loss = pl.pallas_call(
        kernel,
        out_shape=(jax.ShapeDtypeStruct((64, 128), F32), jax.ShapeDtypeStruct((8, 128), F32)),
        in_specs=[anywhere] * 13,
        out_specs=(anywhere, anywhere),
        scratch_shapes=[
            pltpu.VMEM((1, CP), F32),
            pltpu.VMEM((ROWS, D), BF16),
            pltpu.VMEM((96, CP), BF16),
            pltpu.VMEM((2, D, 384), BF16),
            pltpu.VMEM((2, 128, D), BF16),
            pltpu.VMEM((D, 128), BF16),
            pltpu.VMEM((1152, CP), BF16),
            pltpu.VMEM((64, 128), F32),
            pltpu.VMEM((64, 128), jnp.int32),
            pltpu.VMEM((864, W_RIGHT), BF16),
            pltpu.VMEM((576, ROWS), BF16),
            pltpu.VMEM((160, 96), BF16),
            pltpu.VMEM((512, 512), BF16),
            pltpu.VMEM((64, 128), F32),
            pltpu.VMEM((W_RIGHT, D), BF16),
            pltpu.VMEM((256, 1024), BF16),
            pltpu.VMEM((96, 1152), BF16),
            pltpu.VMEM((96, 1024), BF16),
            pltpu.VMEM((2, 432, 128), F32),
            pltpu.VMEM((2, 288, 128), F32),
            pltpu.VMEM((10, 16, 128), F32),
            pltpu.VMEM((2, 288, 1280), BF16),
            pltpu.VMEM((2, 272, 1152), BF16),
            pltpu.VMEM((16, 8, 128), F32),
            pltpu.VMEM((16, 8, 128), F32),
            pltpu.SemaphoreType.DMA((18,)),
            pltpu.SemaphoreType.DMA((7,)),
            pltpu.SemaphoreType.DMA((7,)),
            pltpu.SemaphoreType.DMA,
            pltpu.SemaphoreType.DMA,
            pltpu.SemaphoreType.DMA,
            pltpu.SemaphoreType.DMA,
            pltpu.SemaphoreType.DMA,
            pltpu.VMEM((8, 128), F32),
            pltpu.SemaphoreType.DMA,
        ],
        compiler_params=pltpu.CompilerParams(
            collective_id=0, has_side_effects=True, vmem_limit_bytes=64 * 1024 * 1024
        ),
        name="contact_block",
    )(
        features, conv_weight, out_weight, proj_weight, offset_embed,
        pair_filter_weight.reshape(1152, CP), head_weight.reshape(1, CP), target, cell_mask, *picks,
    )
    pred, loss = pl.pallas_call(
        finish,
        out_shape=(jax.ShapeDtypeStruct((64, 128), F32), jax.ShapeDtypeStruct((1, 1), F32)),
        in_specs=[vmem, vmem],
        out_specs=(vmem, pl.BlockSpec(memory_space=pltpu.SMEM)),
        compiler_params=pltpu.CompilerParams(vmem_limit_bytes=64 * 1024 * 1024),
        name="finish",
    )(pred, loss)
    return pred, loss[0, 0]


def solution(mesh):
    in_specs = (P("diag", None), P(), P(), P(), P("off", None), P(), P(), P("off", "diag"), P("off", "diag"))
    out_specs = (P("off", "diag"), P())
    return jax.shard_map(body, mesh=mesh, in_specs=in_specs, out_specs=out_specs, check_vma=False)
```

time: 49.5 us -> 35 us (0.71)
  local copies, waits for them, and re-layouts: 11.8 us -> 0 us
  between operations: 2.35 us -> 0.64 us
  Pallas kernels: 34.6 us -> 34.1 us
    unnamed x27 -> x0, local copies, waits for them, and re-layouts: 11.8 us -> none
    pallas_call x1, Pallas kernels: 34.6 us -> 32.8 us  [body(): pl.pallas_call(kernel, out_shape=(jax.ShapeDtypeStruct((64, 128), F32), j...]
    pallas_call x0 -> x1, Pallas kernels: none -> 1.4 us  [body(): pl.pallas_call(finish, out_shape=(jax.ShapeDtypeStruct((64, 128), F32), j...]
where the time goes in v2:
time: 35 us; the launch traced here: 34.8 us
  Pallas kernels  34.1 us (97%)
  between operations  0.64 us (2%)
    pallas_call x1, Pallas kernels, body(): pl.pallas_call(kernel, out_shape=(jax.ShapeDtypeStruct((64, 128), F32), j...  32.8 us
    pallas_call x1, Pallas kernels, body(): pl.pallas_call(finish, out_shape=(jax.ShapeDtypeStruct((64, 128), F32), j...  1.4 us

profile of v2, /device:TPU:1, one launch (start us, length us, event | category | flops | bytes accessed | tf_op | source)
XLA Modules:
  0.0 34.8 jit_solution(3155281023428374724)
XLA Ops:
  0.6 32.8 %contact_block.1 = (f32[64,128]{1,0:T(8,128)}, f32[8,128]{1,0:T(8,128)}) custom-call(bf16[128,256]{1,0:T(8,128)(2,1)} %feat.1, bf16[2,3,256,128]{3,2,1,0:T(8,128)(2,1)} %conv.1, bf16[2,128,256]{2,1,0:T(8,128)(2,1)} %outw.1, bf16[256,128]{1,0:T(8,128)(2,1)} %proj.1, bf16[64,64]{1,0:T(8,128)(2,1)} %emb.1, bf16[1152,64]{1,0:T(8,128)(2,1)} %bitcast.3, ...), custom_call_target="tpu_custom_call" | custom-call | tf_op jit(solution)/shard_map/contact_block/pallas_call | solution.py:420
  33.4 1.4 %finish.1 = (f32[64,128]{1,0:T(8,128)}, f32[1,1]{1,0:T(1,128)}) custom-call(f32[64,128]{1,0:T(8,128)} %get-tuple-element.6.pred_in, f32[8,128]{1,0:T(8,128)} %get-tuple-element.7.parts), custom_call_target="tpu_custom_call" | custom-call | tf_op jit(solution)/shard_map/finish/pallas_call | solution.py:470

commit v3 on v2

--- a/solution.py
+++ b/solution.py
@@ -64,8 +64,8 @@
 
     feat_moves = [(0, -1, 96, 0), (1, 1, 0, 160)]
     embed_moves = [(2, -1, 48, 0), (3, 1, 0, 80)]
-    even_moves = [(4, h - 1, 96, 32, 0), (5, h, 0, 128, 32), (6, h + 1, 0, 96, 160)]
-    odd_moves = [(4, h, 32, 96, 0), (5, h + 1, 0, 128, 96), (6, h + 2, 0, 32, 224)]
+    even_moves = [(5, h, 0, 128, 32), (6, h + 1, 0, 96, 160), (4, h - 1, 96, 32, 0)]
+    odd_moves = [(5, h + 1, 0, 128, 96), (4, h, 32, 96, 0), (6, h + 2, 0, 32, 224)]
 
     def on_diag(index):
         return jnp.logical_and(index >= 0, index < N_DIAG)
@@ -126,6 +126,8 @@
     def count_of(cond):
         return jnp.where(cond, 1, 0).astype(jnp.int32)
 
+    for step in z_steps:
+        greet(z_peer(step))
     total = jnp.int32(30)
     for reach in (-1, 1):
         ok = on_diag(d - reach)
@@ -141,8 +143,6 @@
         pl.when(ok_s)(lambda ahead=ahead: greet((d - ahead, g)))
         pl.when(ok_r)(lambda ahead=ahead: greet((d + ahead, g)))
         total = total + count_of(ok_s) + count_of(ok_r)
-    for step in z_steps:
-        greet(z_peer(step))
     for step in xy_steps:
         greet(xy_peer(step))
 
@@ -154,9 +154,9 @@
     for copy in own:
         copy.wait()
     pl.semaphore_wait(barrier, total)
-    each_right(right_begin)
     for one in feat_moves:
         pl.when(on_diag(d - one[1]))(lambda one=one: feat_move(*one).start())
+    each_right(right_begin)
     for one in embed_moves:
         pl.when(on_off(g - one[1]))(lambda one=one: embed_move(*one).start())
 

time: 35 us -> 33.6 us (0.960)
  Pallas kernels: 34.1 us -> 32.8 us
    pallas_call x1, Pallas kernels: 32.8 us -> 31.4 us  [body(): pl.pallas_call(kernel, out_shape=(jax.ShapeDtypeStruct((64, 128), F32), j...]
where the time goes in v3:
time: 33.6 us; the launch traced here: 33.4 us
  Pallas kernels  32.8 us (98%)
  between operations  0.64 us (2%)
    pallas_call x1, Pallas kernels, body(): pl.pallas_call(kernel, out_shape=(jax.ShapeDtypeStruct((64, 128), F32), j...  31.4 us
    pallas_call x1, Pallas kernels, body(): pl.pallas_call(finish, out_shape=(jax.ShapeDtypeStruct((64, 128), F32), j...  1.4 us

profile of v3, /device:TPU:1, one launch (start us, length us, event | category | flops | bytes accessed | tf_op | source)
XLA Modules:
  0.0 33.4 jit_solution(9520060829843478513)
XLA Ops:
  0.6 31.4 %contact_block.1 = (f32[64,128]{1,0:T(8,128)}, f32[8,128]{1,0:T(8,128)}) custom-call(bf16[128,256]{1,0:T(8,128)(2,1)} %feat.1, bf16[2,3,256,128]{3,2,1,0:T(8,128)(2,1)} %conv.1, bf16[2,128,256]{2,1,0:T(8,128)(2,1)} %outw.1, bf16[256,128]{1,0:T(8,128)(2,1)} %proj.1, bf16[64,64]{1,0:T(8,128)(2,1)} %emb.1, bf16[1152,64]{1,0:T(8,128)(2,1)} %bitcast.3, ...), custom_call_target="tpu_custom_call" | custom-call | tf_op jit(solution)/shard_map/contact_block/pallas_call | solution.py:420
  32.0 1.4 %finish.1 = (f32[64,128]{1,0:T(8,128)}, f32[1,1]{1,0:T(1,128)}) custom-call(f32[64,128]{1,0:T(8,128)} %get-tuple-element.6.pred_in, f32[8,128]{1,0:T(8,128)} %get-tuple-element.7.parts), custom_call_target="tpu_custom_call" | custom-call | tf_op jit(solution)/shard_map/finish/pallas_call | solution.py:470

commit v4 on v3

--- a/solution.py
+++ b/solution.py
@@ -48,7 +48,7 @@
     feat, conv, outw, proj, emb, filt, head, target, mask, sel_r, sel_l, sel_e, sel_b,
     pred, loss,
     vhead, win, ewin, wconv, wout, wproj, wfilt, vtarget, vmask, vsel_r, vsel_l, vsel_e, vsel_b, vpred,
-    rwin, first, gin, gpair, rr, ll, ee, pair, inner, red1, red2,
+    rwin, first, gin, gpair, rr, ll, ee, pair, inner, red1,
     local_sem, send_sem, recv_sem, pred_sem, s1, r1, s2, r2, vloss, loss_sem,
 ):
     d = lax.axis_index("diag")
@@ -371,28 +371,25 @@
     valid = jnp.where(o_of + i_of < BINS, vmask[...].astype(F32), 0.0)
     err = valid * (vpred[...] - vtarget[...]) ** 2
 
-    def reduce_over(buf, slot, value, steps, peer, send, recv):
-        buf[slot] = value
+    def spread(source, buf, steps, slot, peer, send, recv):
         for step in steps:
             pltpu.make_async_remote_copy(
-                src_ref=buf.at[slot], dst_ref=buf.at[slot], send_sem=send, recv_sem=recv,
+                src_ref=source, dst_ref=buf.at[slot], send_sem=send, recv_sem=recv,
                 device_id=peer(step), device_id_type=pl.DeviceIdType.MESH,
             ).start()
-        pltpu.make_async_copy(buf.at[pl.ds(0, 15)], buf.at[pl.ds(0, 15)], recv).wait()
-        return jnp.sum(buf[...], axis=0)
-
-    def reduce_retire(buf, send):
-        pltpu.make_async_copy(buf.at[pl.ds(0, 15)], buf.at[pl.ds(0, 15)], send).wait()
-
-    partial = jnp.sum(err.reshape(8, 8, 128), axis=0)
-    partial = reduce_over(red1, z_slot, partial, z_steps, z_peer, s1, r1)
-    partial = reduce_over(red2, xy_slot, partial, xy_steps, xy_peer, s2, r2)
-    vloss[...] = partial
-    loss_copy = pltpu.make_async_copy(vloss, loss, loss_sem)
-    loss_copy.start()
+
+    def settled(buf, sem):
+        pltpu.make_async_copy(buf.at[pl.ds(0, 15)], buf.at[pl.ds(0, 15)], sem).wait()
+
+    red1[z_slot] = jnp.sum(err, axis=0, keepdims=True)
+    spread(red1.at[z_slot], red1, z_steps, z_slot, z_peer, s1, r1)
+    settled(red1, r1)
+    vloss[...] = jnp.sum(red1[...], axis=0)
+    spread(vloss, loss, xy_steps, xy_slot, xy_peer, s2, r2)
+    own_part = pltpu.make_async_copy(vloss, loss.at[xy_slot], loss_sem)
+    own_part.start()
 
     out_copy.wait()
-    loss_copy.wait()
     for one in feat_moves:
         pl.when(on_diag(d - one[1]))(lambda one=one: feat_move(*one).wait_send())
     for one in embed_moves:
@@ -404,8 +401,10 @@
         )
 
     each_right(right_retire)
-    reduce_retire(red1, s1)
-    reduce_retire(red2, s2)
+    settled(red1, s1)
+    settled(loss, s2)
+    own_part.wait()
+    settled(loss, r2)
 
 
 def finish(pred_in, parts, pred, loss):
@@ -419,7 +418,7 @@
     picks = [jnp.asarray(value) for value in selections()]
     pred, loss = pl.pallas_call(
         kernel,
-        out_shape=(jax.ShapeDtypeStruct((64, 128), F32), jax.ShapeDtypeStruct((8, 128), F32)),
+        out_shape=(jax.ShapeDtypeStruct((64, 128), F32), jax.ShapeDtypeStruct((16, 1, 128), F32)),
         in_specs=[anywhere] * 13,
         out_specs=(anywhere, anywhere),
         scratch_shapes=[
@@ -446,8 +445,7 @@
             pltpu.VMEM((10, 16, 128), F32),
             pltpu.VMEM((2, 288, 1280), BF16),
             pltpu.VMEM((2, 272, 1152), BF16),
-            pltpu.VMEM((16, 8, 128), F32),
-            pltpu.VMEM((16, 8, 128), F32),
+            pltpu.VMEM((16, 1, 128), F32),
             pltpu.SemaphoreType.DMA((18,)),
             pltpu.SemaphoreType.DMA((7,)),
             pltpu.SemaphoreType.DMA((7,)),
@@ -456,7 +454,7 @@
             pltpu.SemaphoreType.DMA,
             pltpu.SemaphoreType.DMA,
             pltpu.SemaphoreType.DMA,
-            pltpu.VMEM((8, 128), F32),
+            pltpu.VMEM((1, 128), F32),
             pltpu.SemaphoreType.DMA,
         ],
         compiler_params=pltpu.CompilerParams(

time: 33.6 us -> 32.9 us (0.979)
  Pallas kernels: 32.8 us -> 32 us
    pallas_call x1, Pallas kernels: 31.4 us -> 30.6 us  [body(): pl.pallas_call(kernel, out_shape=(jax.ShapeDtypeStruct((64, 128), F32), j...]
where the time goes in v4:
time: 32.9 us; the launch traced here: 32.7 us
  Pallas kernels  32 us (97%)
  between operations  0.64 us (2%)
    pallas_call x1, Pallas kernels, body(): pl.pallas_call(kernel, out_shape=(jax.ShapeDtypeStruct((64, 128), F32), j...  30.6 us
    pallas_call x1, Pallas kernels, body(): pl.pallas_call(finish, out_shape=(jax.ShapeDtypeStruct((64, 128), F32), j...  1.41 us

profile of v4, /device:TPU:1, one launch (start us, length us, event | category | flops | bytes accessed | tf_op | source)
XLA Modules:
  0.0 32.7 jit_solution(4872795230865750901)
XLA Ops:
  0.6 30.6 %contact_block.1 = (f32[64,128]{1,0:T(8,128)}, f32[16,1,128]{2,1,0:T(1,128)}) custom-call(bf16[128,256]{1,0:T(8,128)(2,1)} %feat.1, bf16[2,3,256,128]{3,2,1,0:T(8,128)(2,1)} %conv.1, bf16[2,128,256]{2,1,0:T(8,128)(2,1)} %outw.1, bf16[256,128]{1,0:T(8,128)(2,1)} %proj.1, bf16[64,64]{1,0:T(8,128)(2,1)} %emb.1, bf16[1152,64]{1,0:T(8,128)(2,1)} %bitcast.3, ...), custom_call_target="tpu_custom_call" | custom-call | tf_op jit(solution)/shard_map/contact_block/pallas_call | solution.py:419
  31.2 1.4 %finish.1 = (f32[64,128]{1,0:T(8,128)}, f32[1,1]{1,0:T(1,128)}) custom-call(f32[64,128]{1,0:T(8,128)} %get-tuple-element.6.pred_in, f32[16,1,128]{2,1,0:T(1,128)} %get-tuple-element.7.parts), custom_call_target="tpu_custom_call" | custom-call | tf_op jit(solution)/shard_map/finish/pallas_call | solution.py:468

commit v5 on v4

--- a/solution.py
+++ b/solution.py
@@ -258,7 +258,9 @@
         copy.wait()
     lane_l = lax.broadcasted_iota(jnp.int32, (ROWS, 128), 1) < 64
     left = jnp.where(lane_l, projected, swapped).astype(BF16)
-    ll[...] = dot(vsel_l[...], left).reshape(2, 288, 128)
+    step_l = lax.broadcasted_iota(jnp.int32, (2, 288, 128), 1) // 16
+    out_l = jnp.logical_or(jnp.logical_and(d == 0, step_l == 0), jnp.logical_and(d == N_DIAG - 1, step_l == 17))
+    ll[...] = jnp.where(out_l, -1e30, dot(vsel_l[...], left).reshape(2, 288, 128))
     for one in embed_moves:
         pl.when(on_off(g + one[1]))(lambda one=one: embed_move(*one).wait_recv())
     erow = lax.broadcasted_iota(jnp.int32, (96, 64), 0) + 64 * g - 16
@@ -266,7 +268,9 @@
     e_val = jnp.where(e_in, ewin[...].astype(F32), 0.0).astype(BF16)
     e_two = dot(e_val, twice)
     e_two = jnp.where(lane96 < 64, e_two, pltpu.roll(e_two, 92, 0)).astype(BF16)
-    ee[...] = dot(vsel_e[...], e_two).reshape(10, 16, 128)
+    step_e = lax.broadcasted_iota(jnp.int32, (10, 16, 128), 0)
+    out_e = jnp.logical_or(jnp.logical_and(g == 0, step_e == 0), jnp.logical_and(g == N_OFF - 1, step_e == 9))
+    ee[...] = jnp.where(out_e, -1e30, dot(vsel_e[...], e_two).reshape(10, 16, 128))
 
     def right_finish(number, ahead, start, count, to):
         pl.when(jnp.logical_and(on_diag(d + ahead), ahead != 0))(
@@ -292,51 +296,23 @@
             value = rr[par, m * 16 : m * 16 + 288, :] + ll[par] + e
             pair[par, :, m * 128 : (m + 1) * 128] = jnp.maximum(value, 0.0).astype(BF16)
 
-    @pl.when(d == 0)
-    def _():
-        pair[:, 0:16, :] = jnp.zeros((2, 16, 1280), BF16)
-
-    @pl.when(d == N_DIAG - 1)
-    def _():
-        pair[:, 272:288, :] = jnp.zeros((2, 16, 1280), BF16)
-
-    @pl.when(g == 0)
-    def _():
-        pair[:, :, 0:128] = jnp.zeros((2, 288, 128), BF16)
-
-    @pl.when(g == N_OFF - 1)
-    def _():
-        pair[:, :, 1152:1280] = jnp.zeros((2, 288, 128), BF16)
-
+    lane_n = lax.broadcasted_iota(jnp.int32, (272, 256), 1) % 128
     for m in range(9):
         cols = slice(m * 128, m * 128 + 256)
         near = jnp.concatenate(
             [pair[0, 0:272, cols], pair[1, 0:272, cols], pair[0, 16:288, cols], pair[1, 16:288, cols]], axis=1
         )
-        acc = jnp.maximum(dot_nt(near, first[...]), 0.0).astype(BF16)
-        inner[0, :, m * 128 : (m + 1) * 128] = acc[:, 0:128]
-        inner[1, :, m * 128 : (m + 1) * 128] = acc[:, 128:256]
-
-    @pl.when(d == 0)
-    def _():
-        inner[0, 0:16, :] = jnp.zeros((16, 1152), BF16)
-
-    @pl.when(d == N_DIAG - 1)
-    def _():
-        inner[1, 256:272, :] = jnp.zeros((16, 1152), BF16)
-
-    lane272 = lax.broadcasted_iota(jnp.int32, (272, 128), 1)
-
-    @pl.when(g == 0)
-    def _():
-        for par in range(2):
-            inner[par, :, 0:128] = jnp.where(lane272 < 64, 0.0, inner[par, :, 0:128].astype(F32)).astype(BF16)
-
-    @pl.when(g == N_OFF - 1)
-    def _():
-        for par in range(2):
-            edge = inner[par, :, 1024:1152].astype(F32)
-            inner[par, :, 1024:1152] = jnp.where(lane272 < 64, edge, 0.0).astype(BF16)
+        acc = jnp.maximum(dot_nt(near, first[...]), 0.0)
+        if m == 0:
+            acc = jnp.where(jnp.logical_and(lane_n < 64, g == 0), 0.0, acc)
+        if m == 8:
+            acc = jnp.where(jnp.logical_and(lane_n >= 64, g == N_OFF - 1), 0.0, acc)
+        acc = acc.astype(BF16)
+        cols = slice(m * 128, (m + 1) * 128)
+        inner[0, 0:16, cols] = jnp.where(d == 0, 0.0, acc[0:16, 0:128].astype(F32)).astype(BF16)
+        inner[0, 16:272, cols] = acc[16:272, 0:128]
+        inner[1, 0:256, cols] = acc[0:256, 128:256]
+        inner[1, 256:272, cols] = jnp.where(d == N_DIAG - 1, 0.0, acc[256:272, 128:256].astype(F32)).astype(BF16)
 
     def turned(value):
         full = jnp.concatenate([value, jnp.zeros((256, 32), F32)], axis=1)

time: 32.9 us -> 32.3 us (0.982)
  Pallas kernels: 32 us -> 31.5 us
    pallas_call x1, Pallas kernels: 30.6 us -> 30.1 us  [body(): pl.pallas_call(kernel, out_shape=(jax.ShapeDtypeStruct((64, 128), F32), j...]
where the time goes in v5:
time: 32.3 us; the launch traced here: 32.1 us
  Pallas kernels  31.5 us (98%)
  between operations  0.64 us (2%)
    pallas_call x1, Pallas kernels, body(): pl.pallas_call(kernel, out_shape=(jax.ShapeDtypeStruct((64, 128), F32), j...  30.1 us
    pallas_call x1, Pallas kernels, body(): pl.pallas_call(finish, out_shape=(jax.ShapeDtypeStruct((64, 128), F32), j...  1.41 us

profile of v5, /device:TPU:1, one launch (start us, length us, event | category | flops | bytes accessed | tf_op | source)
XLA Modules:
  0.0 32.1 jit_solution(6351766959913662599)
XLA Ops:
  0.6 30.1 %contact_block.1 = (f32[64,128]{1,0:T(8,128)}, f32[16,1,128]{2,1,0:T(1,128)}) custom-call(bf16[128,256]{1,0:T(8,128)(2,1)} %feat.1, bf16[2,3,256,128]{3,2,1,0:T(8,128)(2,1)} %conv.1, bf16[2,128,256]{2,1,0:T(8,128)(2,1)} %outw.1, bf16[256,128]{1,0:T(8,128)(2,1)} %proj.1, bf16[64,64]{1,0:T(8,128)(2,1)} %emb.1, bf16[1152,64]{1,0:T(8,128)(2,1)} %bitcast.3, ...), custom_call_target="tpu_custom_call" | custom-call | tf_op jit(solution)/shard_map/contact_block/pallas_call | solution.py:395
  30.7 1.4 %finish.1 = (f32[64,128]{1,0:T(8,128)}, f32[1,1]{1,0:T(1,128)}) custom-call(f32[64,128]{1,0:T(8,128)} %get-tuple-element.6.pred_in, f32[16,1,128]{2,1,0:T(1,128)} %get-tuple-element.7.parts), custom_call_target="tpu_custom_call" | custom-call | tf_op jit(solution)/shard_map/finish/pallas_call | solution.py:444

commit v6 on v5

--- a/solution.py
+++ b/solution.py
@@ -254,6 +254,13 @@
 
     projected, swapped = trunk(win, ROWS, 128 * d - 32)
 
+    def right_own(number, ahead, start, count, to):
+        @pl.when(ahead == 0)
+        def _():
+            rwin[to : to + count, :] = win[32 + start : 32 + start + count, :]
+
+    each_right(right_own)
+
     for copy in copies[10:]:
         copy.wait()
     lane_l = lax.broadcasted_iota(jnp.int32, (ROWS, 128), 1) < 64
@@ -279,12 +286,6 @@
 
     each_right(right_finish)
 
-    def right_own(number, ahead, start, count, to):
-        @pl.when(ahead == 0)
-        def _():
-            rwin[to : to + count, :] = win[32 + start : 32 + start + count, :]
-
-    each_right(right_own)
     projected, swapped = trunk(rwin, W_RIGHT, 128 * d + 64 * g - 32)
     lane_r = lax.broadcasted_iota(jnp.int32, (W_RIGHT, 128), 1) < 64
     right = jnp.where(lane_r, swapped, pltpu.roll(projected, W_RIGHT - 4, 0)).astype(BF16)

time: 32.3 us -> 32.3 us (level)
  no operation moved by 1% of the time
where the time goes in v6:
time: 32.3 us; the launch traced here: 32.1 us
  Pallas kernels  31.5 us (98%)
  between operations  0.64 us (2%)
    pallas_call x1, Pallas kernels, body(): pl.pallas_call(kernel, out_shape=(jax.ShapeDtypeStruct((64, 128), F32), j...  30.1 us
    pallas_call x1, Pallas kernels, body(): pl.pallas_call(finish, out_shape=(jax.ShapeDtypeStruct((64, 128), F32), j...  1.41 us

profile of v6, /device:TPU:1, one launch (start us, length us, event | category | flops | bytes accessed | tf_op | source)
XLA Modules:
  0.0 32.1 jit_solution(4266662529664324093)
XLA Ops:
  0.6 30.1 %contact_block.1 = (f32[64,128]{1,0:T(8,128)}, f32[16,1,128]{2,1,0:T(1,128)}) custom-call(bf16[128,256]{1,0:T(8,128)(2,1)} %feat.1, bf16[2,3,256,128]{3,2,1,0:T(8,128)(2,1)} %conv.1, bf16[2,128,256]{2,1,0:T(8,128)(2,1)} %outw.1, bf16[256,128]{1,0:T(8,128)(2,1)} %proj.1, bf16[64,64]{1,0:T(8,128)(2,1)} %emb.1, bf16[1152,64]{1,0:T(8,128)(2,1)} %bitcast.3, ...), custom_call_target="tpu_custom_call" | custom-call | tf_op jit(solution)/shard_map/contact_block/pallas_call | solution.py:396
  30.7 1.4 %finish.1 = (f32[64,128]{1,0:T(8,128)}, f32[1,1]{1,0:T(1,128)}) custom-call(f32[64,128]{1,0:T(8,128)} %get-tuple-element.6.pred_in, f32[16,1,128]{2,1,0:T(1,128)} %get-tuple-element.7.parts), custom_call_target="tpu_custom_call" | custom-call | tf_op jit(solution)/shard_map/finish/pallas_call | solution.py:445
